TPU v7x, 128 devices: a whole 4x4x4 slice. The times are simulated.
128 devices in a mesh: lon: 32 (over x, z, core), lat: 4 (over y).
Axes of the slice: x: 4, y: 4, z: 4, core: 2. Of those that a mesh axis runs over, the one named last changes fastest.
Arguments:
- tracer: float32 [8, 1280, 4096], P(None, 'lat', 'lon'), may hold values from -6 to 6
- east_vel: float32 [8, 1280, 4096], P(None, 'lat', 'lon'), may hold values from -5 to 5
- north_vel: float32 [8, 1280, 4096], P(None, 'lat', 'lon'), may hold values from -5 to 5
- levels: int32 [1280, 4096], P('lat', 'lon'), may hold values from 0 to 8
- forcing: float32 [1280, 4096], P('lat', 'lon'), may hold values from -8 to 8
- storage: float32 [1280, 4096], P('lat', 'lon'), may hold values from 0.02 to 0.2
Outputs:
- new_tracer: float32 [8, 1280, 4096], P(None, 'lat', 'lon')
- surface: float32 [1280, 4096], P('lat', 'lon')
- residual: float32 [1280, 4096], P('lat', 'lon')
Inputs may be any that keep to these rules, and one draw needn't show every extreme that they name: `levels`: 0 marks land; 8 marks a column wet at every level of the window.
All inputs are finite; a program needn't handle non-finite values.
Results may differ from a plain program's by a relative error of at most 0.0003.
Values sent between devices are 32-bit elements; how exact they have to be, the bound alone decides.
A program may use at most 128 MiB of HBM per device.

v0:
```python
import jax
import jax.numpy as jnp
from jax import lax
from jax.sharding import PartitionSpec as P

ITERS = 5


ADVECT = 0.25
SPREAD = 0.12
VERTICAL = 0.1
CORNER = 0.25
OFFSETS = ((1, 0), (-1, 0), (0, 1), (0, -1), (1, 1), (1, -1), (-1, 1), (-1, -1))


def extended(cells, sides, width):
    for axis, dim in sides:
        count = lax.axis_size(axis)
        head = lax.slice_in_dim(cells, 0, width, axis=dim)
        tail = lax.slice_in_dim(cells, cells.shape[dim] - width, cells.shape[dim], axis=dim)
        cells = jnp.concatenate(
            [
                lax.ppermute(tail, axis, [(i, (i + 1) % count) for i in range(count)]),
                cells,
                lax.ppermute(head, axis, [((i + 1) % count, i) for i in range(count)]),
            ],
            axis=dim,
        )
    return cells


def mirror_rows(source):
    col_count = source.shape[1]
    gathered = lax.all_gather(source, "lon", axis=1, tiled=True)
    flipped = gathered[:, ::-1]
    offset = lax.axis_index("lon") * col_count
    return lax.dynamic_slice_in_dim(flipped, offset, col_count, 1)


def neighbour(padded, step_lat, step_lon):
    row_count = padded.shape[-2] - 2
    col_count = padded.shape[-1] - 2
    return padded[
        ..., 1 + step_lat : 1 + step_lat + row_count, 1 + step_lon : 1 + step_lon + col_count
    ]


def tendency(padded, not_top):
    temp_pad, wet_pad, east_pad, north_pad = (padded[0], padded[1], padded[2], padded[3])
    temp_mid = neighbour(temp_pad, 0, 0)
    temp_east = neighbour(temp_pad, 0, 1)
    temp_west = neighbour(temp_pad, 0, -1)
    temp_north = neighbour(temp_pad, 1, 0)
    temp_south = neighbour(temp_pad, -1, 0)
    wet_mid = neighbour(wet_pad, 0, 0)
    open_east = wet_mid * neighbour(wet_pad, 0, 1)
    open_west = wet_mid * neighbour(wet_pad, 0, -1)
    open_north = wet_mid * neighbour(wet_pad, 1, 0)
    open_south = wet_mid * neighbour(wet_pad, -1, 0)
    vel_mid = neighbour(east_pad, 0, 0)
    flux_east = 0.25 * (vel_mid + neighbour(east_pad, 0, 1)) * open_east * (temp_mid + temp_east)
    flux_west = 0.25 * (neighbour(east_pad, 0, -1) + vel_mid) * open_west * (temp_west + temp_mid)
    merid_mid = neighbour(north_pad, 0, 0)
    flux_north = (
        0.25
        * (merid_mid + neighbour(north_pad, 1, 0))
        * open_north
        * not_top
        * (temp_mid + temp_north)
    )
    flux_south = (
        0.25 * (neighbour(north_pad, -1, 0) + merid_mid) * open_south * (temp_south + temp_mid)
    )
    lateral = (
        open_east * (temp_east - temp_mid)
        + open_west * (temp_west - temp_mid)
        + open_north * (temp_north - temp_mid)
        + open_south * (temp_south - temp_mid)
    )
    zeroes = jnp.zeros_like(temp_mid[:1])
    temp_up = jnp.concatenate([temp_mid[1:], zeroes], axis=0)
    wet_up = jnp.concatenate([wet_mid[1:], zeroes], axis=0)
    temp_down = jnp.concatenate([zeroes, temp_mid[:-1]], axis=0)
    wet_down = jnp.concatenate([zeroes, wet_mid[:-1]], axis=0)
    vertical = wet_mid * wet_up * (temp_up - temp_mid) + wet_mid * wet_down * (temp_down - temp_mid)
    change = (
        ADVECT * (flux_west - flux_east + flux_south - flux_north)
        + SPREAD * lateral
        + VERTICAL * vertical
    )
    return temp_mid + wet_mid * change


def couplings(depth_pad, not_top):
    centre = neighbour(depth_pad, 0, 0)
    result = []
    for step_lat, step_lon in OFFSETS:
        beside = neighbour(depth_pad, step_lat, step_lon)
        weight = centre * beside / (centre + beside + 1.0)
        if step_lat != 0 and step_lon != 0:
            weight = CORNER * weight
        if step_lat == 1 and step_lon != 0:
            weight = weight * not_top
        result.append(weight)
    return result


def surface_rims(source, is_top, is_bottom):
    padded = extended(source, (("lon", 1), ("lat", 0)), 1)
    folded = mirror_rows(source[-1:, :])[0]
    ghost_row = jnp.where(is_top, jnp.pad(folded, 1), padded[-1])
    padded = padded.at[-1].set(ghost_row)
    return padded.at[0].set(jnp.where(is_bottom, jnp.zeros_like(padded[0]), padded[0]))


def local(tracer, east_vel, north_vel, levels, forcing, storage):
    level_count, lat_count, lon_count = tracer.shape
    lat_index = lax.axis_index("lat")
    lat_size = lax.axis_size("lat")
    is_top = lat_index == lat_size - 1
    is_bottom = lat_index == 0
    layer_index = lax.broadcasted_iota(jnp.int32, (level_count, lat_count, lon_count), 0)
    wet_mask = (layer_index < levels[None]).astype(jnp.float32)
    level_float = levels.astype(jnp.float32)
    stacked = jnp.stack([tracer, wet_mask, east_vel, north_vel])
    padded = extended(stacked, (("lon", 3), ("lat", 2)), 1)
    top_rows = jnp.concatenate([tracer[:, -1, :], wet_mask[:, -1, :]], axis=0)
    folded = mirror_rows(top_rows).reshape(2, level_count, lon_count)
    padded = padded.at[:2, :, -1, 1:-1].set(jnp.where(is_top, folded, padded[:2, :, -1, 1:-1]))
    padded = padded.at[:, :, 0, :].set(
        jnp.where(is_bottom, jnp.zeros_like(padded[:, :, 0, :]), padded[:, :, 0, :])
    )
    row_index = lat_index * lat_count + lax.broadcasted_iota(jnp.int32, (lat_count, 1), 0)
    not_top = (row_index < lat_size * lat_count - 1).astype(jnp.float32)
    new_tracer = tendency(padded, not_top)
    column_wet = (levels > 0).astype(jnp.float32)
    right_side = forcing * column_wet + jnp.sum(wet_mask * new_tracer, axis=0) / jnp.sqrt(
        jnp.float32(level_count)
    )
    weights = couplings(surface_rims(level_float, is_top, is_bottom), not_top)
    diagonal = storage
    for weight in weights:
        diagonal = diagonal + weight

    def operate(source):
        rimmed = surface_rims(source, is_top, is_bottom)
        result = diagonal * source
        for (step_lat, step_lon), weight in zip(OFFSETS, weights):
            result = result - weight * neighbour(rimmed, step_lat, step_lon)
        return result

    surface = jnp.zeros_like(right_side)
    residual = right_side

    def precondition(resid):
        scaled = resid / diagonal
        return (scaled, lax.psum(jnp.sum(resid * scaled), ("lon", "lat")))

    scaled, norm_now = precondition(residual)

    def iterate_plain(turn_index, carried):
        surf, resid, direction, norm_old = carried
        image = operate(direction)
        step_size = norm_old / lax.psum(jnp.sum(direction * image), ("lon", "lat"))
        surf = surf + step_size * direction
        resid = resid - step_size * image
        scaled_new, norm_next = precondition(resid)
        direction = scaled_new + norm_next / norm_old * direction
        return (surf, resid, direction, norm_next)

    surface, residual, unused_dir, unused_norm = lax.fori_loop(
        0, ITERS, iterate_plain, (surface, residual, scaled, norm_now)
    )
    return (new_tracer, surface, residual)


def solution(mesh):
    placed = (
        P(None, "lat", "lon"),
        P(None, "lat", "lon"),
        P(None, "lat", "lon"),
        P("lat", "lon"),
        P("lat", "lon"),
        P("lat", "lon"),
    )
    return jax.shard_map(
        local,
        mesh=mesh,
        in_specs=placed,
        out_specs=(P(None, "lat", "lon"), P("lat", "lon"), P("lat", "lon")),
        check_vma=False,
    )
```

profile of v0, /device:TPU:0, one launch (start us, length us, event | category | flops | bytes accessed | tf_op | source)
XLA Modules:
  0.0 1022.6 jit_solution(7794344282848626353)
XLA Ops:
  7.2 5.6 fusion.37
  12.9 3.6 copy.20
  16.5 4.2 copy.21
  20.7 5.8 collective-permute-start.5
  27.3 5.1 collective-permute-start.9
  33.9 17.8 %all_gather.14 = f32[1,4096]{1,0:T(1,128)S(1)} all-gather(f32[1,128]{1,0:T(1,128)S(1)} %slice.470), channel_id=1, replica_groups=mesh['lon'=32,'lat'=4] {'lon'}, dimensions={1}, use_global_device_ids=true | all-gather | bytes 16896 | tf_op jit(solution)/shard_map/all_gather | solution.py:34
  51.7 2.8 rev.14
  55.2 3.0 collective-permute-start.11
  58.2 24.8 %all_gather.13 = f32[16,4096]{1,0:T(8,128)S(1)} all-gather(f32[16,128]{1,0:T(8,128)S(1)} %pad_maximum_fusion.13), channel_id=1, replica_groups=mesh['lon'=32,'lat'=4] {'lon'}, dimensions={1}, use_global_device_ids=true | all-gather | bytes 270336 | tf_op jit(solution)/shard_map/all_gather | solution.py:34
  83.0 10.7 %rev.13 = f32[16,4096]{1,0:T(8,128)} reverse(f32[16,4096]{1,0:T(8,128)S(1)} %all_gather.13), dimensions={1} | reverse | bytes 524288 | tf_op jit(solution)/shard_map/rev | solution.py:35
  93.8 4.7 collective-permute-done.10
  99.8 3.9 copy.22
  103.7 3.8 copy.23
  113.8 13.0 %pad_maximum_fusion.4 = f32[4,8,322,130]{3,1,2,0:T(8,128)} fusion(f32[4,8,1,130]{3,1,2,0:T(8,128)S(1)} %collective-permute-done.7, f32[4,8,320,1]{3,1,2,0:T(8,128)} %copy.23, f32[1,8,320,128]{3,1,2,0:T(8,128)} %copy-done, f32[1,8,320,128]{3,1,2,0:T(8,128)} %copy-done.1, f32[1,8,320,128]{3,1,2,0:T(8,128)S(1)} %fusion.29, f32[1,8,320,128]{3,1,2,0:T(8,128)S(1)} %bitcast.38, ...), kind=kLoop, calls=%fused_computation.28 | loop fusion | flops 9376640 | bytes 10716160 | tf_op jit(solution)/shard_map/concatenate | solution.py:21
  130.6 6.4 slice_bitcast_fusion.1
  136.9 2.2 fusion.38
  139.1 2.2 fusion.39
  141.4 9.2 select_reduce_fusion
  152.6 62.9 %psum.29 = f32[]{:T(128)} all-reduce(f32[]{:T(128)} %get-tuple-element.416), channel_id=1, replica_groups=mesh['lon'=32,'lat'=4] {'lon','lat'}, use_global_device_ids=true, to_apply=%region_2.3 | all-reduce | flops 1 | bytes 8 | tf_op jit(solution)/shard_map/psum | solution.py:157
  215.5 2.6 copy.26
  218.2 803.7 %while.26 = (s32[]{:T(128)}, f32[320,128]{1,0:T(8,128)S(1)}, f32[320,128]{1,0:T(8,128)S(1)}, f32[320,128]{1,0:T(8,128)S(1)}, f32[]{:T(128)}, /*index=5*/f32[320,...) while((s32[]{:T(128)}, f32[320,128]{1,0:T(8,128)S(1)}, ...), condition=%wide.region_8.9_spmd.clone, body=%wide.region_3.0_spmd.clone.sunk | while | flops 1356072 | bytes 5330119 | solution.py:171
  220.0 20.9 %all_gather.17 = f32[1,4096]{1,0:T(1,128)S(1)} all-gather(f32[1,128]{1,0:T(1,128)S(1)} %slice.676), channel_id=1, replica_groups=mesh['lon'=32,'lat'=4] {'lon'}, dimensions={1}, use_global_device_ids=true | all-gather | bytes 16896 | tf_op jit(solution)/shard_map/while/body/eval_jaxpr/all_gather | solution.py:34
  240.9 2.8 rev.17
  247.4 2.3 collective-permute-done.3
  250.9 62.6 %psum.34 = f32[]{:T(128)} all-reduce(f32[]{:T(128)} %get-tuple-element.569), channel_id=1, replica_groups=mesh['lon'=32,'lat'=4] {'lon','lat'}, use_global_device_ids=true, to_apply=%region_5.5 | all-reduce | flops 1 | bytes 8 | tf_op jit(solution)/shard_map/while/body/eval_jaxpr/psum | solution.py:164
  315.0 62.4 %psum.35 = f32[]{:T(128)} all-reduce(f32[]{:T(128)} %get-tuple-element.571), channel_id=1, replica_groups=mesh['lon'=32,'lat'=4] {'lon','lat'}, use_global_device_ids=true, to_apply=%region_7.7 | all-reduce | flops 1 | bytes 8 | tf_op jit(solution)/shard_map/while/body/eval_jaxpr/psum | solution.py:157
  378.3 2.2 collective-permute-start
  380.5 20.9 %all_gather.17 = f32[1,4096]{1,0:T(1,128)S(1)} all-gather(f32[1,128]{1,0:T(1,128)S(1)} %slice.676), channel_id=1, replica_groups=mesh['lon'=32,'lat'=4] {'lon'}, dimensions={1}, use_global_device_ids=true | all-gather | bytes 16896 | tf_op jit(solution)/shard_map/while/body/eval_jaxpr/all_gather | solution.py:34
  401.3 2.8 rev.17
  407.9 2.9 collective-permute-done.3
  412.0 62.4 %psum.34 = f32[]{:T(128)} all-reduce(f32[]{:T(128)} %get-tuple-element.569), channel_id=1, replica_groups=mesh['lon'=32,'lat'=4] {'lon','lat'}, use_global_device_ids=true, to_apply=%region_5.5 | all-reduce | flops 1 | bytes 8 | tf_op jit(solution)/shard_map/while/body/eval_jaxpr/psum | solution.py:164
  475.8 62.7 %psum.35 = f32[]{:T(128)} all-reduce(f32[]{:T(128)} %get-tuple-element.571), channel_id=1, replica_groups=mesh['lon'=32,'lat'=4] {'lon','lat'}, use_global_device_ids=true, to_apply=%region_7.7 | all-reduce | flops 1 | bytes 8 | tf_op jit(solution)/shard_map/while/body/eval_jaxpr/psum | solution.py:157
  539.3 2.2 collective-permute-start
  541.5 20.9 %all_gather.17 = f32[1,4096]{1,0:T(1,128)S(1)} all-gather(f32[1,128]{1,0:T(1,128)S(1)} %slice.676), channel_id=1, replica_groups=mesh['lon'=32,'lat'=4] {'lon'}, dimensions={1}, use_global_device_ids=true | all-gather | bytes 16896 | tf_op jit(solution)/shard_map/while/body/eval_jaxpr/all_gather | solution.py:34
  562.4 2.8 rev.17
  568.9 2.6 collective-permute-done.3
  572.8 62.6 %psum.34 = f32[]{:T(128)} all-reduce(f32[]{:T(128)} %get-tuple-element.569), channel_id=1, replica_groups=mesh['lon'=32,'lat'=4] {'lon','lat'}, use_global_device_ids=true, to_apply=%region_5.5 | all-reduce | flops 1 | bytes 8 | tf_op jit(solution)/shard_map/while/body/eval_jaxpr/psum | solution.py:164
  636.8 62.4 %psum.35 = f32[]{:T(128)} all-reduce(f32[]{:T(128)} %get-tuple-element.571), channel_id=1, replica_groups=mesh['lon'=32,'lat'=4] {'lon','lat'}, use_global_device_ids=true, to_apply=%region_7.7 | all-reduce | flops 1 | bytes 8 | tf_op jit(solution)/shard_map/while/body/eval_jaxpr/psum | solution.py:157
  702.3 20.9 %all_gather.17 = f32[1,4096]{1,0:T(1,128)S(1)} all-gather(f32[1,128]{1,0:T(1,128)S(1)} %slice.676), channel_id=1, replica_groups=mesh['lon'=32,'lat'=4] {'lon'}, dimensions={1}, use_global_device_ids=true | all-gather | bytes 16896 | tf_op jit(solution)/shard_map/while/body/eval_jaxpr/all_gather | solution.py:34
  723.2 2.8 rev.17
  729.7 2.9 collective-permute-done.3
  733.8 62.4 %psum.34 = f32[]{:T(128)} all-reduce(f32[]{:T(128)} %get-tuple-element.569), channel_id=1, replica_groups=mesh['lon'=32,'lat'=4] {'lon','lat'}, use_global_device_ids=true, to_apply=%region_5.5 | all-reduce | flops 1 | bytes 8 | tf_op jit(solution)/shard_map/while/body/eval_jaxpr/psum | solution.py:164
  797.6 62.7 %psum.35 = f32[]{:T(128)} all-reduce(f32[]{:T(128)} %get-tuple-element.571), channel_id=1, replica_groups=mesh['lon'=32,'lat'=4] {'lon','lat'}, use_global_device_ids=true, to_apply=%region_7.7 | all-reduce | flops 1 | bytes 8 | tf_op jit(solution)/shard_map/while/body/eval_jaxpr/psum | solution.py:157
  863.4 20.9 %all_gather.17 = f32[1,4096]{1,0:T(1,128)S(1)} all-gather(f32[1,128]{1,0:T(1,128)S(1)} %slice.676), channel_id=1, replica_groups=mesh['lon'=32,'lat'=4] {'lon'}, dimensions={1}, use_global_device_ids=true | all-gather | bytes 16896 | tf_op jit(solution)/shard_map/while/body/eval_jaxpr/all_gather | solution.py:34
  884.2 2.8 rev.17
  890.8 2.6 collective-permute-done.3
  894.6 62.6 %psum.34 = f32[]{:T(128)} all-reduce(f32[]{:T(128)} %get-tuple-element.569), channel_id=1, replica_groups=mesh['lon'=32,'lat'=4] {'lon','lat'}, use_global_device_ids=true, to_apply=%region_5.5 | all-reduce | flops 1 | bytes 8 | tf_op jit(solution)/shard_map/while/body/eval_jaxpr/psum | solution.py:164
  958.6 62.4 %psum.35 = f32[]{:T(128)} all-reduce(f32[]{:T(128)} %get-tuple-element.571), channel_id=1, replica_groups=mesh['lon'=32,'lat'=4] {'lon','lat'}, use_global_device_ids=true, to_apply=%region_7.7 | all-reduce | flops 1 | bytes 8 | tf_op jit(solution)/shard_map/while/body/eval_jaxpr/psum | solution.py:157
  (149 shorter events, 55.9 us)
Async XLA Ops:
  0.6 2.2 copy-start.3
  0.6 2.4 copy-start.6
  2.9 1.3 copy-start.5
  5.7 1.1 copy-start
  5.7 1.5 copy-start.1
  16.4 83.3 %collective-permute-start.4 = (f32[4,8,320,1]{2,1,3,0:T(8,128)S(1)}, f32[4,8,320,1]{2,1,3,0:T(8,128)}, u32[]{:S(2)}, u32[]{:S(2)}) collective-permute-start(f32[4,8,320,1]{2,1,3,0:T(8,128)S(1)} %copy.20), channel_id=1, source_target_pairs={{0,4},{4,8},{8,12},{12,16},{16,20},{20,24},{24,28},{28,32},{32,36}... | collective-permute-start | bytes 122888 | tf_op jit(solution)/shard_map/ppermute | solution.py:23
  20.7 83.0 %collective-permute-start.5 = (f32[4,8,320,1]{2,1,3,0:T(8,128)}, f32[4,8,320,1]{2,1,3,0:T(8,128)}, u32[]{:S(2)}, u32[]{:S(2)}) collective-permute-start(f32[4,8,320,1]{2,1,3,0:T(8,128)} %copy.21), channel_id=1, source_target_pairs={{4,0},{8,4},{12,8},{16,12},{20,16},{24,20},{28,24},{32,28},{36,32}... | collective-permute-start | bytes 122888 | tf_op jit(solution)/shard_map/ppermute | solution.py:25
  27.3 27.3 %collective-permute-start.8 = (f32[320,1]{1,0:T(8,128)}, f32[320,1]{1,0:T(8,128)S(1)}, u32[]{:S(2)}, u32[]{:S(2)}) collective-permute-start(f32[320,1]{1,0:T(8,128)} %get-tuple-element.452), channel_id=1, source_target_pairs={{0,4},{4,8},{8,12},{12,16},{16,20},{20,24},{24,28},{28,32},{32,36}... | collective-permute-start | bytes 3848 | tf_op jit(solution)/shard_map/ppermute | solution.py:23
  27.3 27.3 %collective-permute-start.9 = (f32[320,1]{1,0:T(8,128)S(1)}, f32[320,1]{1,0:T(8,128)S(1)}, u32[]{:S(2)}, u32[]{:S(2)}) collective-permute-start(f32[320,1]{1,0:T(8,128)S(1)} %get-tuple-element.453), channel_id=1, source_target_pairs={{4,0},{8,4},{12,8},{16,12},{20,16},{24,20},{28,24},{32,28},{36,32}... | collective-permute-start | bytes 3848 | tf_op jit(solution)/shard_map/ppermute | solution.py:25
  54.5 0.7 copy-start.7
  54.5 0.7 copy-start.8
  55.2 38.5 %collective-permute-start.11 = (f32[1,130]{1,0:T(1,128)S(1)}, f32[1,130]{1,0:T(1,128)S(1)}, u32[]{:S(2)}, u32[]{:S(2)}) collective-permute-start(f32[1,130]{1,0:T(1,128)S(1)} %get-tuple-element.451), channel_id=1, source_target_pairs={{1,0},{2,1},{3,2},{0,3},{5,4},{6,5},{7,6},{4,7},{9,8},{10,9},{11,1... | collective-permute-start | bytes 1568 | tf_op jit(solution)/shard_map/ppermute | solution.py:25
  93.7 4.8 collective-permute-start.10
  108.3 4.2 collective-permute-start.7
  108.6 5.2 collective-permute-start.6
  218.3 25.4 %collective-permute-start = (f32[320,1]{1,0:T(8,128)S(1)}, f32[320,1]{1,0:T(8,128)S(1)}, u32[]{:S(2)}, u32[]{:S(2)}) collective-permute-start(f32[320,1]{1,0:T(8,128)S(1)} %get-tuple-element.564), channel_id=1, source_target_pairs={{4,0},{8,4},{12,8},{16,12},{20,16},{24,20},{28,24},{32,28},{36,32}... | collective-permute-start | bytes 3848 | tf_op jit(solution)/shard_map/while/body/eval_jaxpr/ppermute | solution.py:25
  220.0 23.7 %collective-permute-start.1 = (f32[320,1]{1,0:T(8,128)S(1)}, f32[320,1]{1,0:T(8,128)S(1)}, u32[]{:S(2)}, u32[]{:S(2)}) collective-permute-start(f32[320,1]{1,0:T(8,128)S(1)} %get-tuple-element.565), channel_id=1, source_target_pairs={{0,4},{4,8},{8,12},{12,16},{16,20},{20,24},{24,28},{28,32},{32,36}... | collective-permute-start | bytes 3848 | tf_op jit(solution)/shard_map/while/body/eval_jaxpr/ppermute | solution.py:23
  243.7 3.6 collective-permute-start.2
  244.9 4.8 collective-permute-start.3
  378.3 25.9 %collective-permute-start = (f32[320,1]{1,0:T(8,128)S(1)}, f32[320,1]{1,0:T(8,128)S(1)}, u32[]{:S(2)}, u32[]{:S(2)}) collective-permute-start(f32[320,1]{1,0:T(8,128)S(1)} %get-tuple-element.564), channel_id=1, source_target_pairs={{4,0},{8,4},{12,8},{16,12},{20,16},{24,20},{28,24},{32,28},{36,32}... | collective-permute-start | bytes 3848 | tf_op jit(solution)/shard_map/while/body/eval_jaxpr/ppermute | solution.py:25
  380.5 23.7 %collective-permute-start.1 = (f32[320,1]{1,0:T(8,128)S(1)}, f32[320,1]{1,0:T(8,128)S(1)}, u32[]{:S(2)}, u32[]{:S(2)}) collective-permute-start(f32[320,1]{1,0:T(8,128)S(1)} %get-tuple-element.565), channel_id=1, source_target_pairs={{0,4},{4,8},{8,12},{12,16},{16,20},{20,24},{24,28},{28,32},{32,36}... | collective-permute-start | bytes 3848 | tf_op jit(solution)/shard_map/while/body/eval_jaxpr/ppermute | solution.py:23
  404.2 3.6 collective-permute-start.2
  405.9 4.8 collective-permute-start.3
  539.3 25.9 %collective-permute-start = (f32[320,1]{1,0:T(8,128)S(1)}, f32[320,1]{1,0:T(8,128)S(1)}, u32[]{:S(2)}, u32[]{:S(2)}) collective-permute-start(f32[320,1]{1,0:T(8,128)S(1)} %get-tuple-element.564), channel_id=1, source_target_pairs={{4,0},{8,4},{12,8},{16,12},{20,16},{24,20},{28,24},{32,28},{36,32}... | collective-permute-start | bytes 3848 | tf_op jit(solution)/shard_map/while/body/eval_jaxpr/ppermute | solution.py:25
  541.5 23.7 %collective-permute-start.1 = (f32[320,1]{1,0:T(8,128)S(1)}, f32[320,1]{1,0:T(8,128)S(1)}, u32[]{:S(2)}, u32[]{:S(2)}) collective-permute-start(f32[320,1]{1,0:T(8,128)S(1)} %get-tuple-element.565), channel_id=1, source_target_pairs={{0,4},{4,8},{8,12},{12,16},{16,20},{20,24},{24,28},{28,32},{32,36}... | collective-permute-start | bytes 3848 | tf_op jit(solution)/shard_map/while/body/eval_jaxpr/ppermute | solution.py:23
  565.3 3.6 collective-permute-start.2
  566.7 4.8 collective-permute-start.3
  700.1 25.9 %collective-permute-start = (f32[320,1]{1,0:T(8,128)S(1)}, f32[320,1]{1,0:T(8,128)S(1)}, u32[]{:S(2)}, u32[]{:S(2)}) collective-permute-start(f32[320,1]{1,0:T(8,128)S(1)} %get-tuple-element.564), channel_id=1, source_target_pairs={{4,0},{8,4},{12,8},{16,12},{20,16},{24,20},{28,24},{32,28},{36,32}... | collective-permute-start | bytes 3848 | tf_op jit(solution)/shard_map/while/body/eval_jaxpr/ppermute | solution.py:25
  702.3 23.7 %collective-permute-start.1 = (f32[320,1]{1,0:T(8,128)S(1)}, f32[320,1]{1,0:T(8,128)S(1)}, u32[]{:S(2)}, u32[]{:S(2)}) collective-permute-start(f32[320,1]{1,0:T(8,128)S(1)} %get-tuple-element.565), channel_id=1, source_target_pairs={{0,4},{4,8},{8,12},{12,16},{16,20},{20,24},{24,28},{28,32},{32,36}... | collective-permute-start | bytes 3848 | tf_op jit(solution)/shard_map/while/body/eval_jaxpr/ppermute | solution.py:23
  726.1 3.6 collective-permute-start.2
  727.8 4.8 collective-permute-start.3
  861.2 25.9 %collective-permute-start = (f32[320,1]{1,0:T(8,128)S(1)}, f32[320,1]{1,0:T(8,128)S(1)}, u32[]{:S(2)}, u32[]{:S(2)}) collective-permute-start(f32[320,1]{1,0:T(8,128)S(1)} %get-tuple-element.564), channel_id=1, source_target_pairs={{4,0},{8,4},{12,8},{16,12},{20,16},{24,20},{28,24},{32,28},{36,32}... | collective-permute-start | bytes 3848 | tf_op jit(solution)/shard_map/while/body/eval_jaxpr/ppermute | solution.py:25
  863.4 23.7 %collective-permute-start.1 = (f32[320,1]{1,0:T(8,128)S(1)}, f32[320,1]{1,0:T(8,128)S(1)}, u32[]{:S(2)}, u32[]{:S(2)}) collective-permute-start(f32[320,1]{1,0:T(8,128)S(1)} %get-tuple-element.565), channel_id=1, source_target_pairs={{0,4},{4,8},{8,12},{12,16},{16,20},{20,24},{24,28},{28,32},{32,36}... | collective-permute-start | bytes 3848 | tf_op jit(solution)/shard_map/while/body/eval_jaxpr/ppermute | solution.py:23
  887.1 3.6 collective-permute-start.2
  888.5 4.8 collective-permute-start.3
  1021.8 0.7 copy-start.2
  1021.8 0.7 copy-start.4
where the time goes:
time: 1030 us; the launch traced here: 1020 us
  blocking collectives  835 us (81%)
  local copies, waits for them, and re-layouts  72.7 us (7%)
  other arithmetic  41 us (4%)
  starting transfers between devices  37.2 us (4%)
  waiting for transfers between devices  25.3 us (2%)
  loops' own time  10.4 us (1%)
    psum x6, blocking collectives, precondition(): return (scaled, lax.psum(jnp.sum(resid * scaled), ('lon', 'lat')))  376 us
    psum x5, blocking collectives, iterate_plain(): step_size = norm_old / lax.psum(jnp.sum(direction * image), ('lon', 'lat'))  313 us
    all_gather x7, blocking collectives, mirror_rows(): gathered = lax.all_gather(source, 'lon', axis=1, tiled=True)  147 us
    ppermute x14, starting transfers between devices, extended(): lax.ppermute(head, axis, [((i + 1) % count, i) for i in range(count)])  28.7 us
    rev x7, local copies, waits for them, and re-layouts, mirror_rows(): flipped = gathered[:, ::-1]  27.4 us
  transfers between devices with their start and end apart: 28, of which 13 were waited for; matrix products, arithmetic and copies ran while one was open for 4% of the time, Pallas kernels for 0%

commit v1 on v0

v1 whole, which is shorter than its diff:
```python
import functools

import jax
import jax.numpy as jnp
from jax import lax
from jax.experimental import pallas as pl
from jax.experimental.pallas import tpu as pltpu
from jax.sharding import PartitionSpec as P

ITERS = 5
LEVELS = 8
GHOST = 8
BASE = 2 * GHOST
LANES = 128
EDGE = 6
SCALE = 0.8
MESH = pl.DeviceIdType.MESH

GAIN = (-1.0, 1.0 / SCALE, 2.0 / SCALE, 2.0 / SCALE, 2.0 / SCALE)
SHIFT = (1.0, 0.0, 0.0, 0.0, 0.0)
BACK = (0.0, 0.0, SCALE / 2, SCALE / 2, SCALE / 2)
PAIRS = tuple((i, j) for j in range(ITERS + 1) for i in range(j + 1) if (i, j) != (ITERS, ITERS))


def roll(x, shift):
    return pltpu.roll(x, shift % x.shape[-1], x.ndim - 1)


def lane_of(shape):
    return lax.broadcasted_iota(jnp.int32, shape, len(shape) - 1)


def row_of(shape):
    return lax.broadcasted_iota(jnp.int32, shape, len(shape) - 2)


def face_flux(here, there, vel_here, vel_there, shared, level, factor=None):
    carried = (vel_here + vel_there) * (here + there)
    if factor is not None:
        carried = carried * factor
    return jnp.where(shared > level, 1.92 * (there - here) - carried, 0.0)


def ring_east(main, strip, lane):
    a, b = roll(main, -1), roll(strip, -1)
    last = lane == LANES - 1
    return jnp.where(last, b, a), jnp.where(last, a, b)


def ring_west(main, strip, lane):
    a, b = roll(main, 1), roll(strip, 1)
    first = lane == 0
    return jnp.where(first, b, a), jnp.where(first, a, b)


def solve(gram):
    size = ITERS + 1

    def product(left, right):
        total = None
        for i, a in enumerate(left):
            if a is None:
                continue
            inner = None
            for j, b in enumerate(right):
                if b is None:
                    continue
                term = gram[min(i, j), max(i, j)] * b
                inner = term if inner is None else inner + term
            total = a * inner if total is None else total + a * inner
        return total

    def operate(coeffs):
        out = [None] * size

        def add(k, value):
            out[k] = value if out[k] is None else out[k] + value

        for k in range(ITERS):
            if coeffs[k] is None:
                continue
            add(k + 1, coeffs[k] * (-1.0 / GAIN[k]))
            if SHIFT[k] != 1.0:
                add(k, coeffs[k] * (1.0 - SHIFT[k]))
            if BACK[k] != 0.0:
                add(k - 1, coeffs[k] * (-BACK[k]))
        return out

    one = jnp.ones_like(gram[0, 0])
    scaled = [one] + [None] * ITERS
    direction = list(scaled)
    surface = [None] * size
    rho = product(scaled, scaled)
    for turn in range(ITERS):
        image = operate(direction)
        step = rho / product(direction, image)
        for k in range(size):
            if direction[k] is not None:
                move = step * direction[k]
                surface[k] = move if surface[k] is None else surface[k] + move
            if image[k] is not None:
                move = step * image[k]
                scaled[k] = -move if scaled[k] is None else scaled[k] - move
        if turn == ITERS - 1:
            break
        rho_new = product(scaled, scaled)
        ratio = rho_new / rho
        direction = [
            s if d is None else s + ratio * d for s, d in zip(scaled, direction)
        ]
        rho = rho_new
    return surface[:ITERS], scaled


def kernel(
    lon_count, lat_count, rows,
    t_in, u_in, v_in, lev_in, forc_in, stor_in,
    new_out, surf_out, res_out,
    tr, ur, vr, lv, fo, st,
    pk_e, pk_w, rc_w, rc_e,
    ts, us, vs, ls, sn, total,
    nt, w_e, w_n, w_ne, w_nw, w_er, w_ner, w_nwr, rdiag, diag, basis,
    surf, resid, red1, red2,
    in_sem, ghost_send, ghost_recv, strip_send, strip_recv,
    red1_send, red1_recv, red2_send, red2_recv, out_sem,
):
    lon, lat = lax.axis_index("lon"), lax.axis_index("lat")
    is_top = lat == lat_count - 1
    not_bottom = lat > 0
    top = BASE + rows
    south = BASE - GHOST
    own = pl.ds(BASE, rows)
    tile = (8, LANES)
    lane = lane_of(tile)
    row = row_of(tile)
    groups = rows // 8

    fields_in = (t_in, u_in, v_in, lev_in, forc_in, stor_in)
    fields = (tr, ur, vr, lv, fo, st)

    def rows_at(ref, where):
        return ref.at[:, where, :] if len(ref.shape) == 3 else ref.at[where, :]

    loads = [
        pltpu.make_async_copy(src, rows_at(dst, own), in_sem.at[n])
        for n, (src, dst) in enumerate(zip(fields_in, fields))
    ]
    for load in loads:
        load.start()

    east = lax.rem(lon + 1, lon_count)
    west = lax.rem(lon + lon_count - 1, lon_count)
    up_lat = jnp.where(is_top, lat, lat + 1)
    down_lat = jnp.maximum(lat - 1, 0)
    up_lon = jnp.where(is_top, lon_count - 1 - lon, lon)
    fold_e = lax.rem(2 * lon_count - 2 - lon, lon_count)
    fold_w = lax.rem(lon_count - lon, lon_count)
    up_e = jnp.where(is_top, fold_e, east)
    up_w = jnp.where(is_top, fold_w, west)
    self_e = jnp.logical_and(is_top, fold_e == lon)
    self_w = jnp.logical_and(is_top, fold_w == lon)

    core = lax.rem(lon, 2)
    chip = lon // 2
    chips = lon_count // 2
    near = 2 * lat_count
    near_at = lat * 2 + core

    def near_device(index):
        return {"lon": chip * 2 + lax.rem(index, 2), "lat": index // 2}

    def far_device(index):
        return {"lon": index * 2 + core, "lat": lat}

    barrier = pltpu.get_barrier_semaphore()

    def greet(device):
        pl.semaphore_signal(barrier, inc=1, device_id=device, device_id_type=MESH)

    greet({"lon": east, "lat": lat})
    greet({"lon": west, "lat": lat})
    greet({"lon": up_lon, "lat": up_lat})

    @pl.when(jnp.logical_not(self_e))
    def _():
        greet({"lon": up_e, "lat": up_lat})

    @pl.when(jnp.logical_not(self_w))
    def _():
        greet({"lon": up_w, "lat": up_lat})

    @pl.when(not_bottom)
    def _():
        greet({"lon": lon, "lat": down_lat})
        greet({"lon": east, "lat": down_lat})
        greet({"lon": west, "lat": down_lat})

    for j in range(1, near):
        greet(near_device(lax.rem(near_at + j, near)))
    for j in range(1, chips):
        greet(far_device(lax.rem(chip + j, chips)))

    greeted = 3 + near - 1 + chips - 1
    greeted = greeted + jnp.where(self_e, 0, 1) + jnp.where(self_w, 0, 1) + jnp.where(not_bottom, 3, 0)
    pl.semaphore_wait(barrier, greeted)

    last_in = pl.ds(rows - GHOST, GHOST)
    first_in = pl.ds(0, GHOST)
    north_ghost = pl.ds(top, GHOST)
    south_ghost = pl.ds(south, GHOST)
    up_row = pl.multiple_of(jnp.where(is_top, top, south), 8)
    up_slot = jnp.where(is_top, 1, 0)
    ups, downs = [], []
    for n, (src, dst) in enumerate(zip(fields_in, fields)):
        ups.append(pltpu.make_async_remote_copy(
            rows_at(src, last_in), rows_at(dst, pl.ds(up_row, GHOST)),
            ghost_send.at[0, n], ghost_recv.at[up_slot, n],
            device_id={"lon": up_lon, "lat": up_lat}, device_id_type=MESH,
        ))
        downs.append(pltpu.make_async_remote_copy(
            rows_at(src, first_in), rows_at(dst, north_ghost),
            ghost_send.at[1, n], ghost_recv.at[1, n],
            device_id={"lon": lon, "lat": down_lat}, device_id_type=MESH,
        ))
    for copy in ups:
        copy.start()

    @pl.when(not_bottom)
    def _():
        for copy in downs:
            copy.start()

    for load in loads:
        load.wait()

    def pack(r):
        at = pl.ds(r, 8)
        zero = jnp.zeros(tile, jnp.float32)
        parts = {"e": [zero, zero], "w": [zero, zero]}

        def put(which, slot, x):
            here = jnp.logical_and(lane >= slot, lane < slot + 8)
            parts["e"][which] = jnp.where(here, roll(x, slot + EDGE), parts["e"][which])
            parts["w"][which] = jnp.where(here, roll(x, slot + 2), parts["w"][which])

        for k in range(LEVELS):
            put(0, k * 16, tr[k, at, :])
            put(0, k * 16 + 8, ur[k, at, :])
            put(1, k * 16, vr[k, at, :])
        put(1, 8, lv[at, :].astype(jnp.float32))
        put(1, 24, fo[at, :])
        put(1, 40, st[at, :])
        for which in range(2):
            pk_e[which, at, :] = parts["e"][which]
            pk_w[which, at, :] = parts["w"][which]

    def pack_loop(i, carry):
        pack(pl.multiple_of(BASE + i * 8, 8))
        return carry

    lax.fori_loop(0, groups, pack_loop, 0)

    def strip_copy(src, dst, src_rows, dst_rows, slot, recv_slot, to_lon, to_lat):
        return pltpu.make_async_remote_copy(
            src.at[:, src_rows, :], dst.at[:, dst_rows, :],
            strip_send.at[slot], strip_recv.at[recv_slot],
            device_id={"lon": to_lon, "lat": to_lat}, device_id_type=MESH,
        )

    last_own = pl.ds(top - GHOST, GHOST)
    first_own = pl.ds(BASE, GHOST)
    go_e = strip_copy(pk_e, rc_w, own, own, 0, 0, east, lat)
    go_w = strip_copy(pk_w, rc_e, own, own, 1, 1, west, lat)
    up_e_plain = strip_copy(pk_e, rc_w, last_own, south_ghost, 2, 2, up_e, up_lat)
    up_w_plain = strip_copy(pk_w, rc_e, last_own, south_ghost, 3, 3, up_w, up_lat)
    up_e_fold = strip_copy(pk_e, rc_e, last_own, north_ghost, 2, 5, up_e, up_lat)
    up_w_fold = strip_copy(pk_w, rc_w, last_own, north_ghost, 3, 4, up_w, up_lat)
    up_e_self = pltpu.make_async_copy(
        pk_e.at[:, last_own, :], rc_e.at[:, north_ghost, :], strip_recv.at[5])
    up_w_self = pltpu.make_async_copy(
        pk_w.at[:, last_own, :], rc_w.at[:, north_ghost, :], strip_recv.at[4])
    down_e = strip_copy(pk_e, rc_w, first_own, north_ghost, 4, 4, east, down_lat)
    down_w = strip_copy(pk_w, rc_e, first_own, north_ghost, 5, 5, west, down_lat)
    go_e.start()
    go_w.start()
    fold_e_sent = jnp.logical_and(is_top, jnp.logical_not(self_e))
    fold_w_sent = jnp.logical_and(is_top, jnp.logical_not(self_w))

    @pl.when(jnp.logical_not(is_top))
    def _():
        up_e_plain.start()
        up_w_plain.start()

    @pl.when(fold_e_sent)
    def _():
        up_e_fold.start()

    @pl.when(fold_w_sent)
    def _():
        up_w_fold.start()

    @pl.when(self_e)
    def _():
        up_e_self.start()

    @pl.when(self_w)
    def _():
        up_w_self.start()

    @pl.when(not_bottom)
    def _():
        down_e.start()
        down_w.start()

    fold_row = jnp.where(is_top, top - 1, -1)

    def tracer_rows(r, edge):
        at, up, down = pl.ds(r, 8), pl.ds(r + 1, 8), pl.ds(r - 1, 8)
        depth = lv[at, :]
        open_e = jnp.minimum(depth, roll(depth, -1))
        open_n = jnp.minimum(depth, lv[up, :])
        open_s = jnp.minimum(depth, lv[down, :])
        factor_n = factor_s = None
        if edge:
            factor_n = jnp.where(row + r == fold_row, 0.0, 1.0)
            factor_s = jnp.where(row + (r - 1) == fold_row, 0.0, 1.0)
        below = None
        summed = None
        here = tr[0, at, :]
        for k in range(LEVELS):
            vel = vr[k, at, :]
            zonal = ur[k, at, :]
            flux_e = face_flux(here, roll(here, -1), zonal, roll(zonal, -1), open_e, k)
            flux_n = face_flux(here, tr[k, up, :], vel, vr[k, up, :], open_n, k, factor_n)
            flux_s = face_flux(tr[k, down, :], here, vr[k, down, :], vel, open_s, k, factor_s)
            change = 0.0625 * ((flux_e - roll(flux_e, 1)) + (flux_n - flux_s))
            result = here + change
            if below is not None:
                result = result - below
            if k + 1 < LEVELS:
                above = tr[k + 1, at, :]
                below = jnp.where(depth > k + 1, 0.1 * (above - here), 0.0)
                result = result + below
                here = above
            nt[k, at, :] = result
            wet_part = jnp.where(depth > k, result, 0.0)
            summed = wet_part if summed is None else summed + wet_part
        total[at, :] = summed

    def inner_loop(i, carry):
        tracer_rows(pl.multiple_of(BASE + 8 + i * 8, 8), False)
        return carry

    lax.fori_loop(0, groups - 2, inner_loop, 0)

    @pl.when(not_bottom)
    def _():
        for n, dst in enumerate(fields):
            part = rows_at(dst, south_ghost)
            pltpu.make_async_copy(part, part, ghost_recv.at[0, n]).wait()
        for n, dst in ((2, rc_w), (3, rc_e)):
            part = dst.at[:, south_ghost, :]
            pltpu.make_async_copy(part, part, strip_recv.at[n]).wait()

    for n, dst in enumerate(fields):
        part = rows_at(dst, north_ghost)
        pltpu.make_async_copy(part, part, ghost_recv.at[1, n]).wait()
    for n, dst in ((4, rc_w), (5, rc_e)):
        part = dst.at[:, north_ghost, :]
        pltpu.make_async_copy(part, part, strip_recv.at[n]).wait()

    @pl.when(jnp.logical_not(not_bottom))
    def _():
        for dst in fields + (rc_w, rc_e):
            if len(dst.shape) == 3:
                dst[:, south_ghost, :] = jnp.zeros((dst.shape[0], GHOST, LANES), dst.dtype)
            else:
                dst[south_ghost, :] = jnp.zeros((GHOST, LANES), dst.dtype)

    def swap(x, bit, axis):
        size = x.shape[axis]
        index = lax.broadcasted_iota(jnp.int32, x.shape, axis)
        low = (index // bit) % 2 == 0
        return jnp.where(low, pltpu.roll(x, size - bit, axis), pltpu.roll(x, bit, axis))

    def mirror(x, bits):
        for bit in bits:
            x = swap(x, bit, 1)
        for bit in (1, 2, 4):
            x = swap(x, bit, 0)
        return x

    @pl.when(is_top)
    def _():
        bits = (1, 2, 4, 8, 16, 32, 64)
        at = north_ghost
        for k in range(LEVELS):
            tr[k, at, :] = mirror(tr[k, at, :], bits)
            ur[k, at, :] = -mirror(ur[k, at, :], bits)
            vr[k, at, :] = -mirror(vr[k, at, :], bits)
        for dst in (lv, fo, st):
            dst[at, :] = mirror(dst[at, :], bits)
        field = (lane // 8) % 2
        for dst in (rc_w, rc_e):
            a = mirror(dst[0, at, :], (1, 2, 4))
            b = mirror(dst[1, at, :], (1, 2, 4))
            dst[0, at, :] = jnp.where(field == 1, -a, a)
            dst[1, at, :] = jnp.where(field == 0, -b, b)

    pack(south)
    pack(top)
    for r in (south, BASE, top - 8, top):
        tracer_rows(r, True)

    for n, dst in ((0, rc_w), (1, rc_e)):
        part = dst.at[:, own, :]
        pltpu.make_async_copy(part, part, strip_recv.at[n]).wait()

    column = lane % 8
    side = (lane // 8) % 2
    slab = lane // 16

    def strip_fields(i, carry):
        r = pl.multiple_of(south + i * 8, 8)
        at = pl.ds(r, 8)
        both = []
        for which in range(2):
            a = jnp.where(column >= EDGE, roll(pk_w[which, at, :], 4), rc_w[which, at, :])
            b = jnp.where(column < 2, roll(pk_e[which, at, :], -4), rc_e[which, at, :])
            both.append((a, b))
        (a_w, a_e), (b_w, b_e) = both
        ts[at, :] = jnp.where(side == 0, a_w, roll(a_e, 8))
        us[at, :] = jnp.where(side == 0, roll(a_w, -8), a_e)
        vs[at, :] = jnp.where(side == 0, b_w, roll(b_e, 8))
        extra = jnp.where(side == 0, roll(b_w, -8), b_e)
        depth = jnp.where(slab == 0, extra, 0.0)
        for shift in (16, 32, 64):
            depth = depth + roll(depth, shift)
        ls[at, :] = depth

        def place(x):
            return jnp.where(
                lane < EDGE, roll(x, -10), jnp.where(lane >= LANES - EDGE, roll(x, -6), 0.0))

        basis[0, 1, at, :] = place(roll(extra, -16))
        rdiag[1, at, :] = place(roll(extra, -32))
        basis[1, 1, at, :] = place(extra)
        return carry

    lax.fori_loop(0, groups + 2, strip_fields, 0)

    level = slab.astype(jnp.float32)

    def strip_tracer(i, carry):
        r = pl.multiple_of(south + i * 8, 8)
        at, up, down = pl.ds(r, 8), pl.ds(r + 1, 8), pl.ds(r - 1, 8)
        factor_n = jnp.where(row + r == fold_row, 0.0, 1.0)
        factor_s = jnp.where(row + (r - 1) == fold_row, 0.0, 1.0)
        depth, here, zonal, vel = ls[at, :], ts[at, :], us[at, :], vs[at, :]
        open_e = jnp.minimum(depth, roll(depth, -1))
        open_n = jnp.minimum(depth, ls[up, :])
        open_s = jnp.minimum(depth, ls[down, :])
        flux_e = face_flux(here, roll(here, -1), zonal, roll(zonal, -1), open_e, level)
        flux_n = face_flux(here, ts[up, :], vel, vs[up, :], open_n, level, factor_n)
        flux_s = face_flux(ts[down, :], here, vs[down, :], vel, open_s, level, factor_s)
        change = 0.0625 * ((flux_e - roll(flux_e, 1)) + (flux_n - flux_s))
        rise = jnp.where(
            jnp.logical_and(slab < LEVELS - 1, depth > level + 1.0),
            0.1 * (roll(here, -16) - here), 0.0)
        fall = jnp.where(slab > 0, roll(rise, 16), 0.0)
        result = here + change + rise - fall
        wet_part = jnp.where(depth > level, result, 0.0)
        for shift in (16, 32, 64):
            wet_part = wet_part + roll(wet_part, shift)

        def beside(x):
            return jnp.where(lane % 16 == 5, roll(x, -4), x)

        ends = jnp.logical_or(lane == 0, lane == LANES - 1)
        packed = beside(result)
        for k in range(LEVELS):
            nt[k, at, :] = jnp.where(ends, roll(packed, -(k * 16 + 6)), nt[k, at, :])
        summed = jnp.where(ends, roll(beside(wet_part), -6), total[at, :])
        root = 8.0 ** -0.5
        main_depth = lv[at, :]
        basis[0, 0, at, :] = jnp.where(main_depth > 0, fo[at, :], 0.0) + summed * root

        def place(x):
            return jnp.where(
                lane < EDGE, roll(x, -10), jnp.where(lane >= LANES - EDGE, roll(x, -6), 0.0))

        wet = basis[1, 1, at, :] > 0.0
        basis[0, 1, at, :] = jnp.where(wet, basis[0, 1, at, :], 0.0) + place(wet_part) * root
        basis[1, 0, at, :] = main_depth.astype(jnp.float32)
        return carry

    lax.fori_loop(0, groups + 2, strip_tracer, 0)

    out_new = pltpu.make_async_copy(nt.at[:, own, :], new_out, out_sem.at[0])
    out_new.start()

    def weigh(a, b):
        return a * b / (a + b + 1.0)

    def weights_loop(i, carry):
        r = pl.multiple_of(south + i * 8, 8)
        at, up = pl.ds(r, 8), pl.ds(r + 1, 8)
        d_m, d_s = basis[1, 0, at, :], basis[1, 1, at, :]
        n_m, n_s = basis[1, 0, up, :], basis[1, 1, up, :]
        e_m, e_s = ring_east(d_m, d_s, lane)
        ne_m, ne_s = ring_east(n_m, n_s, lane)
        nw_m, nw_s = ring_west(n_m, n_s, lane)
        corner = jnp.where(row + r == fold_row, 0.0, 0.25)
        east_m, east_s = weigh(d_m, e_m), weigh(d_s, e_s)
        neast_m, neast_s = corner * weigh(d_m, ne_m), corner * weigh(d_s, ne_s)
        nwest_m, nwest_s = corner * weigh(d_m, nw_m), corner * weigh(d_s, nw_s)
        w_e[0, at, :], w_e[1, at, :] = east_m, east_s
        w_n[0, at, :], w_n[1, at, :] = weigh(d_m, n_m), weigh(d_s, n_s)
        w_ne[0, at, :], w_ne[1, at, :] = neast_m, neast_s
        w_nw[0, at, :], w_nw[1, at, :] = nwest_m, nwest_s
        w_er[0, at, :], w_er[1, at, :] = ring_west(east_m, east_s, lane)
        w_ner[0, at, :], w_ner[1, at, :] = ring_west(neast_m, neast_s, lane)
        w_nwr[0, at, :], w_nwr[1, at, :] = ring_east(nwest_m, nwest_s, lane)
        return carry

    lax.fori_loop(0, groups + 2, weights_loop, 0)

    def diagonal_loop(i, carry):
        r = pl.multiple_of(south + i * 8, 8)
        at, down = pl.ds(r, 8), pl.ds(r - 1, 8)
        for half in range(2):
            storage = st[at, :] if half == 0 else rdiag[1, at, :]
            whole = (
                storage + w_e[half, at, :] + w_er[half, at, :] + w_n[half, at, :]
                + w_n[half, down, :] + w_ne[half, at, :] + w_nw[half, at, :]
                + w_ner[half, down, :] + w_nwr[half, down, :])
            inverse = jnp.where(whole > 0.0, 1.0 / whole, 0.0)
            rdiag[half, at, :] = inverse
            if half == 0:
                diag[at, :] = whole
            basis[0, half, at, :] = basis[0, half, at, :] * inverse
        return carry

    lax.fori_loop(0, groups + 2, diagonal_loop, 0)

    gram = {}

    def neighbours_sum(k, r):
        at, up, down = pl.ds(r, 8), pl.ds(r + 1, 8), pl.ds(r - 1, 8)
        sums, to_west, to_east = [], [], []
        for half in range(2):
            x = basis[k, half, at, :]
            x_n = basis[k, half, up, :]
            x_s = basis[k, half, down, :]
            to_east.append(
                w_e[half, at, :] * x + w_ne[half, down, :] * x_s + w_nwr[half, at, :] * x_n)
            to_west.append(
                w_er[half, at, :] * x + w_nw[half, down, :] * x_s + w_ner[half, at, :] * x_n)
            sums.append(w_n[half, at, :] * x_n + w_n[half, down, :] * x_s)
        from_west = ring_west(to_east[0], to_east[1], lane)
        from_east = ring_east(to_west[0], to_west[1], lane)
        return [sums[h] + from_west[h] + from_east[h] for h in range(2)]

    def apply_rows(k, r):
        at = pl.ds(r, 8)
        sums = neighbours_sum(k, r)
        out = []
        for half in range(2):
            x = basis[k, half, at, :]
            y = rdiag[half, at, :] * sums[half]
            if SHIFT[k] != 0.0:
                y = y - SHIFT[k] * x
            if BACK[k] != 0.0:
                y = y - BACK[k] * basis[k - 1, half, at, :]
            y = GAIN[k] * y
            basis[k + 1, half, at, :] = y
            out.append(y)
        return out[0]

    zero = jnp.zeros(tile, jnp.float32)

    def first_gram(i, acc):
        at = pl.ds(pl.multiple_of(BASE + i * 8, 8), 8)
        x = basis[0, 0, at, :]
        return acc + diag[at, :] * x * x

    gram[0, 0] = lax.fori_loop(0, groups, first_gram, zero)
    for k in range(ITERS):
        if k < ITERS - 1:
            apply_rows(k, south)
            apply_rows(k, top)
        terms = [p for p in PAIRS if p[1] == k + 1]

        def apply_loop(i, accs, k=k, terms=terms):
            r = pl.multiple_of(BASE + i * 8, 8)
            at = pl.ds(r, 8)
            y = apply_rows(k, r)
            scaled = diag[at, :] * y
            return tuple(
                acc + scaled * (y if a == k + 1 else basis[a, 0, at, :])
                for acc, (a, _) in zip(accs, terms))

        sums = lax.fori_loop(0, groups, apply_loop, tuple(zero for _ in terms))
        for p, s in zip(terms, sums):
            gram[p] = s

    per_lane = [jnp.sum(gram[p], axis=0, keepdims=True) for p in PAIRS]
    per_lane = per_lane + [jnp.zeros((1, LANES), jnp.float32)] * (24 - len(per_lane))
    stacked = jnp.sum(jnp.concatenate(per_lane, axis=0), axis=1, keepdims=True)
    third = lane // 42
    folded = jnp.where(
        third == 0, stacked[0:8], jnp.where(third == 1, stacked[8:16], stacked[16:24]))

    red1[pl.ds(near_at, 1), :, :] = folded[None]
    sends = []
    for j in range(1, near):
        sends.append(pltpu.make_async_remote_copy(
            red1.at[near_at], red1.at[near_at],
            red1_send.at[j], red1_recv.at[near_at],
            device_id=near_device(lax.rem(near_at + j, near)), device_id_type=MESH,
        ))
    for copy in sends:
        copy.start()
    for j in range(1, near):
        other = lax.rem(near_at + j, near)
        part = red1.at[other]
        pltpu.make_async_copy(part, part, red1_recv.at[other]).wait()
    folded = red1[0]
    for j in range(1, near):
        folded = folded + red1[j]

    red2[pl.ds(chip, 1), :, :] = folded[None]
    far_sends = []
    for j in range(1, chips):
        far_sends.append(pltpu.make_async_remote_copy(
            red2.at[chip], red2.at[chip],
            red2_send.at[j], red2_recv.at[chip],
            device_id=far_device(lax.rem(chip + j, chips)), device_id_type=MESH,
        ))
    for copy in far_sends:
        copy.start()
    for j in range(1, chips):
        other = lax.rem(chip + j, chips)
        part = red2.at[other]
        pltpu.make_async_copy(part, part, red2_recv.at[other]).wait()
    folded = red2[0]
    for j in range(1, chips):
        folded = folded + red2[j]

    sums = {}
    for third_at in range(3):
        spread = jnp.sum(
            jnp.where(lane == third_at * 42, folded, 0.0), axis=1, keepdims=True)
        for n, p in enumerate(PAIRS):
            if n // 8 == third_at:
                sums[p] = jnp.broadcast_to(spread[n % 8:n % 8 + 1], tile)
    surface_by, scaled_by = solve(sums)

    def final_loop(i, carry):
        r = pl.multiple_of(i * 8, 8)
        at = pl.ds(pl.multiple_of(BASE + r, 8), 8)
        x = [basis[k, 0, at, :] for k in range(ITERS + 1)]
        level_at = surface_by[0] * x[0]
        left = scaled_by[0] * x[0]
        for k in range(1, ITERS + 1):
            if k < ITERS:
                level_at = level_at + surface_by[k] * x[k]
            left = left + scaled_by[k] * x[k]
        surf[pl.ds(r, 8), :] = level_at
        resid[pl.ds(r, 8), :] = diag[at, :] * left
        return carry

    lax.fori_loop(0, groups, final_loop, 0)
    out_surf = pltpu.make_async_copy(surf, surf_out, out_sem.at[1])
    out_res = pltpu.make_async_copy(resid, res_out, out_sem.at[2])
    out_surf.start()
    out_res.start()

    for copy in ups:
        copy.wait_send()
    go_e.wait_send()
    go_w.wait_send()

    @pl.when(not_bottom)
    def _():
        for copy in downs:
            copy.wait_send()
        down_e.wait_send()
        down_w.wait_send()

    @pl.when(jnp.logical_not(is_top))
    def _():
        up_e_plain.wait_send()
        up_w_plain.wait_send()

    @pl.when(fold_e_sent)
    def _():
        up_e_fold.wait_send()

    @pl.when(fold_w_sent)
    def _():
        up_w_fold.wait_send()

    for copy in sends + far_sends:
        copy.wait_send()
    out_new.wait()
    out_surf.wait()
    out_res.wait()


def local(lon_count, lat_count, tracer, east_vel, north_vel, levels, forcing, storage):
    rows = tracer.shape[1]
    padded = rows + 4 * GHOST
    flat = (padded, LANES)
    f32 = jnp.float32
    near, chips = 2 * lat_count, lon_count // 2

    def vmem(*shape, dtype=f32):
        return pltpu.VMEM(shape, dtype)

    cube = vmem(LEVELS, *flat)
    pair = vmem(2, *flat)
    plain = vmem(*flat)
    dma = pltpu.SemaphoreType.DMA
    anywhere = pl.BlockSpec(memory_space=pl.ANY)
    return pl.pallas_call(
        functools.partial(kernel, lon_count, lat_count, rows),
        out_shape=(
            jax.ShapeDtypeStruct(tracer.shape, f32),
            jax.ShapeDtypeStruct(levels.shape, f32),
            jax.ShapeDtypeStruct(levels.shape, f32),
        ),
        in_specs=[anywhere] * 6,
        out_specs=(anywhere,) * 3,
        scratch_shapes=[
            cube, cube, cube, vmem(*flat, dtype=jnp.int32), plain, plain,
            pair, pair, pair, pair,
            plain, plain, plain, plain, plain, plain,
            cube, pair, pair, pair, pair, pair, pair, pair, pair, plain,
            vmem(ITERS + 1, 2, *flat),
            vmem(rows, LANES), vmem(rows, LANES),
            vmem(near, 8, LANES), vmem(chips, 8, LANES),
            dma((6,)), dma((2, 6)), dma((2, 6)), dma((6,)), dma((6,)),
            dma((near,)), dma((near,)), dma((chips,)), dma((chips,)), dma((3,)),
        ],
        compiler_params=pltpu.CompilerParams(
            collective_id=0, has_side_effects=True, vmem_limit_bytes=40 * 2**20
        ),
        cost_estimate=pl.CostEstimate(flops=10**8, bytes_accessed=6 * 10**6, transcendentals=0),
        name="ocean_step",
    )(tracer, east_vel, north_vel, levels, forcing, storage)


def solution(mesh):
    cube, flat = P(None, "lat", "lon"), P("lat", "lon")
    return jax.shard_map(
        functools.partial(local, mesh.shape["lon"], mesh.shape["lat"]),
        mesh=mesh,
        in_specs=(cube, cube, cube, flat, flat, flat),
        out_specs=(cube, flat, flat),
        check_vma=False,
    )
```

time: 1030 us -> 105 us (0.10)
  blocking collectives: 835 us -> 0 us
  Pallas kernels: 0 us -> 94.5 us
  local copies, waits for them, and re-layouts: 72.7 us -> 9.08 us
  other arithmetic: 41 us -> 0 us
  starting transfers between devices: 37.2 us -> 0 us
  waiting for transfers between devices: 25.3 us -> 0 us
  loops' own time: 10.4 us -> 0 us
    psum x11 -> x0, blocking collectives: 688 us -> none  [the longest x6 376 us: precondition(): return (scaled, lax.psum(jnp.sum(resid * scaled), ('lon', 'lat')))]
    all_gather x7 -> x0, blocking collectives: 147 us -> none  [mirror_rows(): gathered = lax.all_gather(source, 'lon', axis=1, tiled=True)]
    pallas_call x0 -> x1, Pallas kernels: none -> 94.5 us  [local(): pl.pallas_call(functools.partial(kernel, lon_count, lat_count, rows), out...]
    ppermute x28 -> x0, starting transfers between devices: 37.2 us -> none  [the longest x14 28.7 us: extended(): lax.ppermute(head, axis, [((i + 1) % count, i) for i in range(count)])]
    rev x7 -> x0, local copies, waits for them, and re-layouts: 27.4 us -> none  [mirror_rows(): flipped = gathered[:, ::-1]]
    ppermute x28 -> x0, waiting for transfers between devices: 25.3 us -> none  [the longest x14 19.4 us: extended(): lax.ppermute(tail, axis, [(i, (i + 1) % count) for i in range(count)])]
    reduce_sum x12 -> x0, other arithmetic: 19.4 us -> none  [the longest x1 9.19 us: local(): jnp.sum(wet_mask * new_tracer, axis=0) / jnp.sqrt(jnp.float32(level_count))]
    slice x17 -> x0, local copies, waits for them, and re-layouts: 19.1 us -> none  [the longest x8 10.5 us: extended(): lax.slice_in_dim(cells, cells.shape[dim] - width, cells.shape[dim], axis=...]
  transfers between devices with their start and end apart: 28 -> 0, of which waited for: 13 -> 0; matrix products, arithmetic and copies ran while one was open for 4% -> 0% of each run, Pallas kernels for 0% -> 0%
where the time goes in v1:
time: 105 us; the launch traced here: 104 us
  Pallas kernels  94.5 us (90%)
  local copies, waits for them, and re-layouts  9.08 us (9%)
    pallas_call x1, Pallas kernels, local(): pl.pallas_call(functools.partial(kernel, lon_count, lat_count, rows), out...  94.5 us
    unnamed x15, local copies, waits for them, and re-layouts  9.08 us

profile of v1, /device:TPU:0, one launch (start us, length us, event | category | flops | bytes accessed | tf_op | source)
XLA Modules:
  0.0 104.3 jit_solution(936506892289707979)
XLA Ops:
  0.6 0.0 copy-start
  0.6 1.3 %copy-done = f32[8,320,128]{2,1,0:T(8,128)S(1)} copy-done((f32[8,320,128]{2,1,0:T(8,128)S(1)}, f32[8,320,128]{2,1,0:T(8,128)}, u32[]{:S(2)}) %copy-start) | copy-done | bytes 1310744
  1.9 0.0 copy-start.1
  2.0 1.3 %copy-done.1 = f32[8,320,128]{2,1,0:T(8,128)S(1)} copy-done((f32[8,320,128]{2,1,0:T(8,128)S(1)}, f32[8,320,128]{2,1,0:T(8,128)}, u32[]{:S(2)}) %copy-start.1) | copy-done | bytes 1310744
  3.3 0.0 copy-start.2
  3.3 1.3 %copy-done.2 = f32[8,320,128]{2,1,0:T(8,128)S(1)} copy-done((f32[8,320,128]{2,1,0:T(8,128)S(1)}, f32[8,320,128]{2,1,0:T(8,128)}, u32[]{:S(2)}) %copy-start.2) | copy-done | bytes 1310744
  4.6 0.0 copy-start.3
  4.6 0.9 copy-done.3
  5.5 0.0 copy-start.4
  5.5 0.9 copy-done.4
  6.4 0.0 copy-start.5
  6.4 0.9 copy-done.5
  7.3 94.5 %ocean_step.1 = (f32[8,320,128]{2,1,0:T(8,128)S(1)}, f32[320,128]{1,0:T(8,128)S(1)}, f32[320,128]{1,0:T(8,128)S(1)}) custom-call(f32[8,320,128]{2,1,0:T(8,128)S(1)} %copy-done, f32[8,320,128]{2,1,0:T(8,128)S(1)} %copy-done.1, f32[8,320,128]{2,1,0:T(8,128)S(1)} %copy-done.2, s32[320,128]{1,0:T(8,128)S(1)} %copy-done.3, f32[320,128]{1,0:T(8,128)S(1)} %copy-done.4, ...), custom_call_target="tpu_custom_call" | custom-call | flops 100000000 | bytes 6000000 | tf_op jit(solution)/shard_map/ocean_step/pallas_call | solution.py:726
  101.9 1.1 %copy.12 = f32[8,320,128]{2,1,0:T(8,128)} copy(f32[8,320,128]{2,1,0:T(8,128)S(1)} %get-tuple-element.6) | data formatting | bytes 2621440
  102.9 0.7 copy.13
  103.6 0.7 copy.14
Async XLA Ops:
  0.6 1.3 %copy-start = (f32[8,320,128]{2,1,0:T(8,128)S(1)}, f32[8,320,128]{2,1,0:T(8,128)}, u32[]{:S(2)}) copy-start(f32[8,320,128]{2,1,0:T(8,128)} %t_in.1) | copy-start | bytes 3932164
  1.9 1.3 %copy-start.1 = (f32[8,320,128]{2,1,0:T(8,128)S(1)}, f32[8,320,128]{2,1,0:T(8,128)}, u32[]{:S(2)}) copy-start(f32[8,320,128]{2,1,0:T(8,128)} %u_in.1) | copy-start | bytes 3932164
  3.3 1.3 %copy-start.2 = (f32[8,320,128]{2,1,0:T(8,128)S(1)}, f32[8,320,128]{2,1,0:T(8,128)}, u32[]{:S(2)}) copy-start(f32[8,320,128]{2,1,0:T(8,128)} %v_in.1) | copy-start | bytes 3932164
  4.6 0.9 copy-start.3
  5.5 0.9 copy-start.4
  6.4 0.9 copy-start.5

commit v2 on v1

--- a/solution.py
+++ b/solution.py
@@ -15,6 +15,15 @@
 EDGE = 6
 SCALE = 0.8
 MESH = pl.DeviceIdType.MESH
+PACK_STEP = 40
+TRACER_STEP = 16
+FIELDS_STEP = 112
+STRIPS_STEP = 48
+WEIGHTS_STEP = 48
+DIAGONAL_STEP = 48
+GRAM_STEP = 80
+APPLY_STEP = 40
+FINAL_STEP = 40
 
 GAIN = (-1.0, 1.0 / SCALE, 2.0 / SCALE, 2.0 / SCALE, 2.0 / SCALE)
 SHIFT = (1.0, 0.0, 0.0, 0.0, 0.0)
@@ -32,6 +41,31 @@
 
 def row_of(shape):
     return lax.broadcasted_iota(jnp.int32, shape, len(shape) - 2)
+
+
+def sweep(name, first, rows, step, body, start=0):
+    whole = rows // step
+
+    def chunk(i, carry):
+        return body(pl.multiple_of(first + i * step, 8), step, carry)
+
+    carry = lax.fori_loop(0, whole, chunk, start) if whole else start
+    if rows % step:
+        carry = body(first + whole * step, rows % step, carry)
+    return carry
+
+
+def remote(name, src, dst, sent, received, device):
+    return pltpu.make_async_remote_copy(
+        src, dst, sent, received, device_id=device, device_id_type=MESH)
+
+
+def local_copy(name, src, dst, done):
+    return pltpu.make_async_copy(src, dst, done)
+
+
+def arrived(name, part, received):
+    pltpu.make_async_copy(part, part, received).wait()
 
 
 def face_flux(here, there, vel_here, vel_there, shared, level, factor=None):
@@ -133,7 +167,13 @@
     tile = (8, LANES)
     lane = lane_of(tile)
     row = row_of(tile)
-    groups = rows // 8
+    reach = rows + 2 * GHOST
+
+    def lanes(n):
+        return lane_of((n, LANES))
+
+    def row_is(r, n, which):
+        return row_of((n, LANES)) + r == which
 
     fields_in = (t_in, u_in, v_in, lev_in, forc_in, stor_in)
     fields = (tr, ur, vr, lv, fo, st)
@@ -212,15 +252,13 @@
     up_slot = jnp.where(is_top, 1, 0)
     ups, downs = [], []
     for n, (src, dst) in enumerate(zip(fields_in, fields)):
-        ups.append(pltpu.make_async_remote_copy(
-            rows_at(src, last_in), rows_at(dst, pl.ds(up_row, GHOST)),
-            ghost_send.at[0, n], ghost_recv.at[up_slot, n],
-            device_id={"lon": up_lon, "lat": up_lat}, device_id_type=MESH,
+        ups.append(remote(
+            "halo", rows_at(src, last_in), rows_at(dst, pl.ds(up_row, GHOST)),
+            ghost_send.at[0, n], ghost_recv.at[up_slot, n], {"lon": up_lon, "lat": up_lat},
         ))
-        downs.append(pltpu.make_async_remote_copy(
-            rows_at(src, first_in), rows_at(dst, north_ghost),
-            ghost_send.at[1, n], ghost_recv.at[1, n],
-            device_id={"lon": lon, "lat": down_lat}, device_id_type=MESH,
+        downs.append(remote(
+            "halo", rows_at(src, first_in), rows_at(dst, north_ghost),
+            ghost_send.at[1, n], ghost_recv.at[1, n], {"lon": lon, "lat": down_lat},
         ))
     for copy in ups:
         copy.start()
@@ -233,9 +271,10 @@
     for load in loads:
         load.wait()
 
-    def pack(r):
-        at = pl.ds(r, 8)
-        zero = jnp.zeros(tile, jnp.float32)
+    def pack(r, n, carry=0):
+        at = pl.ds(r, n)
+        lane = lanes(n)
+        zero = jnp.zeros((n, LANES), jnp.float32)
         parts = {"e": [zero, zero], "w": [zero, zero]}
 
         def put(which, slot, x):
@@ -253,18 +292,14 @@
         for which in range(2):
             pk_e[which, at, :] = parts["e"][which]
             pk_w[which, at, :] = parts["w"][which]
-
-    def pack_loop(i, carry):
-        pack(pl.multiple_of(BASE + i * 8, 8))
         return carry
 
-    lax.fori_loop(0, groups, pack_loop, 0)
+    sweep("pack", BASE, rows, PACK_STEP, pack)
 
     def strip_copy(src, dst, src_rows, dst_rows, slot, recv_slot, to_lon, to_lat):
-        return pltpu.make_async_remote_copy(
-            src.at[:, src_rows, :], dst.at[:, dst_rows, :],
-            strip_send.at[slot], strip_recv.at[recv_slot],
-            device_id={"lon": to_lon, "lat": to_lat}, device_id_type=MESH,
+        return remote(
+            "halo", src.at[:, src_rows, :], dst.at[:, dst_rows, :],
+            strip_send.at[slot], strip_recv.at[recv_slot], {"lon": to_lon, "lat": to_lat},
         )
 
     last_own = pl.ds(top - GHOST, GHOST)
@@ -275,10 +310,10 @@
     up_w_plain = strip_copy(pk_w, rc_e, last_own, south_ghost, 3, 3, up_w, up_lat)
     up_e_fold = strip_copy(pk_e, rc_e, last_own, north_ghost, 2, 5, up_e, up_lat)
     up_w_fold = strip_copy(pk_w, rc_w, last_own, north_ghost, 3, 4, up_w, up_lat)
-    up_e_self = pltpu.make_async_copy(
-        pk_e.at[:, last_own, :], rc_e.at[:, north_ghost, :], strip_recv.at[5])
-    up_w_self = pltpu.make_async_copy(
-        pk_w.at[:, last_own, :], rc_w.at[:, north_ghost, :], strip_recv.at[4])
+    up_e_self = local_copy(
+        "halo", pk_e.at[:, last_own, :], rc_e.at[:, north_ghost, :], strip_recv.at[5])
+    up_w_self = local_copy(
+        "halo", pk_w.at[:, last_own, :], rc_w.at[:, north_ghost, :], strip_recv.at[4])
     down_e = strip_copy(pk_e, rc_w, first_own, north_ghost, 4, 4, east, down_lat)
     down_w = strip_copy(pk_w, rc_e, first_own, north_ghost, 5, 5, west, down_lat)
     go_e.start()
@@ -314,16 +349,16 @@
 
     fold_row = jnp.where(is_top, top - 1, -1)
 
-    def tracer_rows(r, edge):
-        at, up, down = pl.ds(r, 8), pl.ds(r + 1, 8), pl.ds(r - 1, 8)
+    def tracer_rows(r, n, edge):
+        at, up, down = pl.ds(r, n), pl.ds(r + 1, n), pl.ds(r - 1, n)
         depth = lv[at, :]
         open_e = jnp.minimum(depth, roll(depth, -1))
         open_n = jnp.minimum(depth, lv[up, :])
         open_s = jnp.minimum(depth, lv[down, :])
         factor_n = factor_s = None
         if edge:
-            factor_n = jnp.where(row + r == fold_row, 0.0, 1.0)
-            factor_s = jnp.where(row + (r - 1) == fold_row, 0.0, 1.0)
+            factor_n = jnp.where(row_is(r, n, fold_row), 0.0, 1.0)
+            factor_s = jnp.where(row_is(r - 1, n, fold_row), 0.0, 1.0)
         below = None
         summed = None
         here = tr[0, at, :]
@@ -347,27 +382,27 @@
             summed = wet_part if summed is None else summed + wet_part
         total[at, :] = summed
 
-    def inner_loop(i, carry):
-        tracer_rows(pl.multiple_of(BASE + 8 + i * 8, 8), False)
+    def inner_rows(r, n, carry):
+        tracer_rows(r, n, False)
         return carry
 
-    lax.fori_loop(0, groups - 2, inner_loop, 0)
+    sweep("tracer", BASE + 8, rows - 16, TRACER_STEP, inner_rows)
 
     @pl.when(not_bottom)
     def _():
         for n, dst in enumerate(fields):
             part = rows_at(dst, south_ghost)
-            pltpu.make_async_copy(part, part, ghost_recv.at[0, n]).wait()
+            arrived("halo", part, ghost_recv.at[0, n])
         for n, dst in ((2, rc_w), (3, rc_e)):
             part = dst.at[:, south_ghost, :]
-            pltpu.make_async_copy(part, part, strip_recv.at[n]).wait()
+            arrived("halo", part, strip_recv.at[n])
 
     for n, dst in enumerate(fields):
         part = rows_at(dst, north_ghost)
-        pltpu.make_async_copy(part, part, ghost_recv.at[1, n]).wait()
+        arrived("halo", part, ghost_recv.at[1, n])
     for n, dst in ((4, rc_w), (5, rc_e)):
         part = dst.at[:, north_ghost, :]
-        pltpu.make_async_copy(part, part, strip_recv.at[n]).wait()
+        arrived("halo", part, strip_recv.at[n])
 
     @pl.when(jnp.logical_not(not_bottom))
     def _():
@@ -407,22 +442,24 @@
             dst[0, at, :] = jnp.where(field == 1, -a, a)
             dst[1, at, :] = jnp.where(field == 0, -b, b)
 
-    pack(south)
-    pack(top)
-    for r in (south, BASE, top - 8, top):
-        tracer_rows(r, True)
+    pack(south, GHOST)
+    pack(top, GHOST)
+    tracer_rows(south, 16, True)
+    tracer_rows(top - 8, 16, True)
 
     for n, dst in ((0, rc_w), (1, rc_e)):
         part = dst.at[:, own, :]
-        pltpu.make_async_copy(part, part, strip_recv.at[n]).wait()
-
-    column = lane % 8
-    side = (lane // 8) % 2
-    slab = lane // 16
-
-    def strip_fields(i, carry):
-        r = pl.multiple_of(south + i * 8, 8)
-        at = pl.ds(r, 8)
+        arrived("halo", part, strip_recv.at[n])
+
+    def place(x):
+        lane = lanes(x.shape[0])
+        return jnp.where(
+            lane < EDGE, roll(x, -10), jnp.where(lane >= LANES - EDGE, roll(x, -6), 0.0))
+
+    def strip_fields(r, n, carry):
+        at = pl.ds(r, n)
+        lane = lanes(n)
+        column, side, slab = lane % 8, (lane // 8) % 2, lane // 16
         both = []
         for which in range(2):
             a = jnp.where(column >= EDGE, roll(pk_w[which, at, :], 4), rc_w[which, at, :])
@@ -437,25 +474,20 @@
         for shift in (16, 32, 64):
             depth = depth + roll(depth, shift)
         ls[at, :] = depth
-
-        def place(x):
-            return jnp.where(
-                lane < EDGE, roll(x, -10), jnp.where(lane >= LANES - EDGE, roll(x, -6), 0.0))
-
         basis[0, 1, at, :] = place(roll(extra, -16))
         rdiag[1, at, :] = place(roll(extra, -32))
         basis[1, 1, at, :] = place(extra)
         return carry
 
-    lax.fori_loop(0, groups + 2, strip_fields, 0)
-
-    level = slab.astype(jnp.float32)
-
-    def strip_tracer(i, carry):
-        r = pl.multiple_of(south + i * 8, 8)
-        at, up, down = pl.ds(r, 8), pl.ds(r + 1, 8), pl.ds(r - 1, 8)
-        factor_n = jnp.where(row + r == fold_row, 0.0, 1.0)
-        factor_s = jnp.where(row + (r - 1) == fold_row, 0.0, 1.0)
+    sweep("fields", south, reach, FIELDS_STEP, strip_fields)
+
+    def strip_tracer(r, n, carry):
+        at, up, down = pl.ds(r, n), pl.ds(r + 1, n), pl.ds(r - 1, n)
+        lane = lanes(n)
+        slab = lane // 16
+        level = slab.astype(jnp.float32)
+        factor_n = jnp.where(row_is(r, n, fold_row), 0.0, 1.0)
+        factor_s = jnp.where(row_is(r - 1, n, fold_row), 0.0, 1.0)
         depth, here, zonal, vel = ls[at, :], ts[at, :], us[at, :], vs[at, :]
         open_e = jnp.minimum(depth, roll(depth, -1))
         open_n = jnp.minimum(depth, ls[up, :])
@@ -484,17 +516,12 @@
         root = 8.0 ** -0.5
         main_depth = lv[at, :]
         basis[0, 0, at, :] = jnp.where(main_depth > 0, fo[at, :], 0.0) + summed * root
-
-        def place(x):
-            return jnp.where(
-                lane < EDGE, roll(x, -10), jnp.where(lane >= LANES - EDGE, roll(x, -6), 0.0))
-
         wet = basis[1, 1, at, :] > 0.0
         basis[0, 1, at, :] = jnp.where(wet, basis[0, 1, at, :], 0.0) + place(wet_part) * root
         basis[1, 0, at, :] = main_depth.astype(jnp.float32)
         return carry
 
-    lax.fori_loop(0, groups + 2, strip_tracer, 0)
+    sweep("strips", south, reach, STRIPS_STEP, strip_tracer)
 
     out_new = pltpu.make_async_copy(nt.at[:, own, :], new_out, out_sem.at[0])
     out_new.start()
@@ -502,15 +529,15 @@
     def weigh(a, b):
         return a * b / (a + b + 1.0)
 
-    def weights_loop(i, carry):
-        r = pl.multiple_of(south + i * 8, 8)
-        at, up = pl.ds(r, 8), pl.ds(r + 1, 8)
+    def weights_rows(r, n, carry):
+        at, up = pl.ds(r, n), pl.ds(r + 1, n)
+        lane = lanes(n)
         d_m, d_s = basis[1, 0, at, :], basis[1, 1, at, :]
         n_m, n_s = basis[1, 0, up, :], basis[1, 1, up, :]
         e_m, e_s = ring_east(d_m, d_s, lane)
         ne_m, ne_s = ring_east(n_m, n_s, lane)
         nw_m, nw_s = ring_west(n_m, n_s, lane)
-        corner = jnp.where(row + r == fold_row, 0.0, 0.25)
+        corner = jnp.where(row_is(r, n, fold_row), 0.0, 0.25)
         east_m, east_s = weigh(d_m, e_m), weigh(d_s, e_s)
         neast_m, neast_s = corner * weigh(d_m, ne_m), corner * weigh(d_s, ne_s)
         nwest_m, nwest_s = corner * weigh(d_m, nw_m), corner * weigh(d_s, nw_s)
@@ -523,11 +550,10 @@
         w_nwr[0, at, :], w_nwr[1, at, :] = ring_east(nwest_m, nwest_s, lane)
         return carry
 
-    lax.fori_loop(0, groups + 2, weights_loop, 0)
-
-    def diagonal_loop(i, carry):
-        r = pl.multiple_of(south + i * 8, 8)
-        at, down = pl.ds(r, 8), pl.ds(r - 1, 8)
+    sweep("weights", south, reach, WEIGHTS_STEP, weights_rows)
+
+    def diagonal_rows(r, n, carry):
+        at, down = pl.ds(r, n), pl.ds(r - 1, n)
         for half in range(2):
             storage = st[at, :] if half == 0 else rdiag[1, at, :]
             whole = (
@@ -541,12 +567,13 @@
             basis[0, half, at, :] = basis[0, half, at, :] * inverse
         return carry
 
-    lax.fori_loop(0, groups + 2, diagonal_loop, 0)
+    sweep("diagonal", south, reach, DIAGONAL_STEP, diagonal_rows)
 
     gram = {}
 
-    def neighbours_sum(k, r):
-        at, up, down = pl.ds(r, 8), pl.ds(r + 1, 8), pl.ds(r - 1, 8)
+    def neighbours_sum(k, r, n):
+        at, up, down = pl.ds(r, n), pl.ds(r + 1, n), pl.ds(r - 1, n)
+        lane = lanes(n)
         sums, to_west, to_east = [], [], []
         for half in range(2):
             x = basis[k, half, at, :]
@@ -561,9 +588,9 @@
         from_east = ring_east(to_west[0], to_west[1], lane)
         return [sums[h] + from_west[h] + from_east[h] for h in range(2)]
 
-    def apply_rows(k, r):
-        at = pl.ds(r, 8)
-        sums = neighbours_sum(k, r)
+    def apply_rows(k, r, n):
+        at = pl.ds(r, n)
+        sums = neighbours_sum(k, r, n)
         out = []
         for half in range(2):
             x = basis[k, half, at, :]
@@ -579,28 +606,30 @@
 
     zero = jnp.zeros(tile, jnp.float32)
 
-    def first_gram(i, acc):
-        at = pl.ds(pl.multiple_of(BASE + i * 8, 8), 8)
+    def fold_rows(x):
+        return jnp.sum(x.reshape(x.shape[0] // 8, 8, LANES), axis=0)
+
+    def first_gram(r, n, acc):
+        at = pl.ds(r, n)
         x = basis[0, 0, at, :]
-        return acc + diag[at, :] * x * x
-
-    gram[0, 0] = lax.fori_loop(0, groups, first_gram, zero)
+        return acc + fold_rows(diag[at, :] * x * x)
+
+    gram[0, 0] = sweep("gram", BASE, rows, GRAM_STEP, first_gram, zero)
     for k in range(ITERS):
         if k < ITERS - 1:
-            apply_rows(k, south)
-            apply_rows(k, top)
+            apply_rows(k, south, GHOST)
+            apply_rows(k, top, GHOST)
         terms = [p for p in PAIRS if p[1] == k + 1]
 
-        def apply_loop(i, accs, k=k, terms=terms):
-            r = pl.multiple_of(BASE + i * 8, 8)
-            at = pl.ds(r, 8)
-            y = apply_rows(k, r)
+        def apply_own(r, n, accs, k=k, terms=terms):
+            at = pl.ds(r, n)
+            y = apply_rows(k, r, n)
             scaled = diag[at, :] * y
             return tuple(
-                acc + scaled * (y if a == k + 1 else basis[a, 0, at, :])
+                acc + fold_rows(scaled * (y if a == k + 1 else basis[a, 0, at, :]))
                 for acc, (a, _) in zip(accs, terms))
 
-        sums = lax.fori_loop(0, groups, apply_loop, tuple(zero for _ in terms))
+        sums = sweep("apply", BASE, rows, APPLY_STEP, apply_own, tuple(zero for _ in terms))
         for p, s in zip(terms, sums):
             gram[p] = s
 
@@ -614,17 +643,16 @@
     red1[pl.ds(near_at, 1), :, :] = folded[None]
     sends = []
     for j in range(1, near):
-        sends.append(pltpu.make_async_remote_copy(
-            red1.at[near_at], red1.at[near_at],
-            red1_send.at[j], red1_recv.at[near_at],
-            device_id=near_device(lax.rem(near_at + j, near)), device_id_type=MESH,
+        sends.append(remote(
+            "red", red1.at[near_at], red1.at[near_at],
+            red1_send.at[j], red1_recv.at[near_at], near_device(lax.rem(near_at + j, near)),
         ))
     for copy in sends:
         copy.start()
     for j in range(1, near):
         other = lax.rem(near_at + j, near)
         part = red1.at[other]
-        pltpu.make_async_copy(part, part, red1_recv.at[other]).wait()
+        arrived("red", part, red1_recv.at[other])
     folded = red1[0]
     for j in range(1, near):
         folded = folded + red1[j]
@@ -632,17 +660,16 @@
     red2[pl.ds(chip, 1), :, :] = folded[None]
     far_sends = []
     for j in range(1, chips):
-        far_sends.append(pltpu.make_async_remote_copy(
-            red2.at[chip], red2.at[chip],
-            red2_send.at[j], red2_recv.at[chip],
-            device_id=far_device(lax.rem(chip + j, chips)), device_id_type=MESH,
+        far_sends.append(remote(
+            "red", red2.at[chip], red2.at[chip],
+            red2_send.at[j], red2_recv.at[chip], far_device(lax.rem(chip + j, chips)),
         ))
     for copy in far_sends:
         copy.start()
     for j in range(1, chips):
         other = lax.rem(chip + j, chips)
         part = red2.at[other]
-        pltpu.make_async_copy(part, part, red2_recv.at[other]).wait()
+        arrived("red", part, red2_recv.at[other])
     folded = red2[0]
     for j in range(1, chips):
         folded = folded + red2[j]
@@ -656,9 +683,12 @@
                 sums[p] = jnp.broadcast_to(spread[n % 8:n % 8 + 1], tile)
     surface_by, scaled_by = solve(sums)
 
-    def final_loop(i, carry):
-        r = pl.multiple_of(i * 8, 8)
-        at = pl.ds(pl.multiple_of(BASE + r, 8), 8)
+    surface_by = [c[0:1] for c in surface_by]
+    scaled_by = [c[0:1] for c in scaled_by]
+
+    def final_rows(r, n, carry):
+        at = pl.ds(r, n)
+        to = pl.ds(pl.multiple_of(r - BASE, 8), n)
         x = [basis[k, 0, at, :] for k in range(ITERS + 1)]
         level_at = surface_by[0] * x[0]
         left = scaled_by[0] * x[0]
@@ -666,11 +696,11 @@
             if k < ITERS:
                 level_at = level_at + surface_by[k] * x[k]
             left = left + scaled_by[k] * x[k]
-        surf[pl.ds(r, 8), :] = level_at
-        resid[pl.ds(r, 8), :] = diag[at, :] * left
+        surf[to, :] = level_at
+        resid[to, :] = diag[at, :] * left
         return carry
 
-    lax.fori_loop(0, groups, final_loop, 0)
+    sweep("final", BASE, rows, FINAL_STEP, final_rows)
     out_surf = pltpu.make_async_copy(surf, surf_out, out_sem.at[1])
     out_res = pltpu.make_async_copy(resid, res_out, out_sem.at[2])
     out_surf.start()
@@ -744,7 +774,7 @@
             dma((near,)), dma((near,)), dma((chips,)), dma((chips,)), dma((3,)),
         ],
         compiler_params=pltpu.CompilerParams(
-            collective_id=0, has_side_effects=True, vmem_limit_bytes=40 * 2**20
+            collective_id=0, has_side_effects=True, vmem_limit_bytes=60 * 2**20
         ),
         cost_estimate=pl.CostEstimate(flops=10**8, bytes_accessed=6 * 10**6, transcendentals=0),
         name="ocean_step",

time: 105 us -> 45.8 us (0.44)
  Pallas kernels: 94.5 us -> 41 us
  local copies, waits for them, and re-layouts: 9.08 us -> 3.85 us
    pallas_call x1, Pallas kernels: 94.5 us -> 41 us  [local(): pl.pallas_call(functools.partial(kernel, lon_count, lat_count, rows), out...]
    unnamed x15 -> x7, local copies, waits for them, and re-layouts: 9.08 us -> 3.85 us
where the time goes in v2:
time: 45.8 us; the launch traced here: 45.5 us
  Pallas kernels  41 us (90%)
  local copies, waits for them, and re-layouts  3.85 us (8%)
  between operations  0.66 us (1%)
    pallas_call x1, Pallas kernels, local(): pl.pallas_call(functools.partial(kernel, lon_count, lat_count, rows), out...  41 us
    unnamed x7, local copies, waits for them, and re-layouts  3.85 us

profile of v2, /device:TPU:0, one launch (start us, length us, event | category | flops | bytes accessed | tf_op | source)
XLA Modules:
  0.0 45.5 jit_solution(7247405061637942111)
XLA Ops:
  0.6 41.0 %ocean_step.1 = (f32[8,320,128]{2,1,0:T(8,128)}, f32[320,128]{1,0:T(8,128)}, f32[320,128]{1,0:T(8,128)}) custom-call(f32[8,320,128]{2,1,0:T(8,128)} %t_in.1, f32[8,320,128]{2,1,0:T(8,128)} %u_in.1, f32[8,320,128]{2,1,0:T(8,128)} %v_in.1, s32[320,128]{1,0:T(8,128)} %lev_in.1, f32[320,128]{1,0:T(8,128)} %forc_in.1, f32[320,128]{1,0:T(8,128)} %stor_in.1), custom_call_target="tpu_custom_call" | custom-call | flops 100000000 | bytes 6000000 | tf_op jit(solution)/shard_map/ocean_step/pallas_call | solution.py:756
  41.6 0.0 copy-start.1
  41.6 0.0 copy-start
  41.6 2.5 %copy.12 = f32[8,320,128]{2,1,0:T(8,128)} copy(f32[8,320,128]{2,1,0:T(8,128)} %get-tuple-element.6) | data formatting | bytes 2621440
  44.2 0.0 copy-done.1
  44.2 0.7 %copy.13 = f32[320,128]{1,0:T(8,128)} copy(f32[320,128]{1,0:T(8,128)S(1)} %copy-done.1) | data formatting | bytes 327680
  44.8 0.0 copy-done
  44.8 0.7 %copy.14 = f32[320,128]{1,0:T(8,128)} copy(f32[320,128]{1,0:T(8,128)S(1)} %copy-done) | data formatting | bytes 327680
Async XLA Ops:
  41.6 2.5 %copy-start.1 = (f32[320,128]{1,0:T(8,128)S(1)}, f32[320,128]{1,0:T(8,128)}, u32[]{:S(2)}) copy-start(f32[320,128]{1,0:T(8,128)} %get-tuple-element.7) | copy-start | bytes 491524
  41.6 3.2 %copy-start = (f32[320,128]{1,0:T(8,128)S(1)}, f32[320,128]{1,0:T(8,128)}, u32[]{:S(2)}) copy-start(f32[320,128]{1,0:T(8,128)} %get-tuple-element.8) | copy-start | bytes 491524

commit v3 on v2

v3 whole, which is shorter than its diff:
```python
import functools

import jax
import jax.numpy as jnp
from jax import lax
from jax.experimental import pallas as pl
from jax.experimental.pallas import tpu as pltpu
from jax.sharding import PartitionSpec as P

ITERS = 5
LEVELS = 8
GHOST = 8
BASE = 2 * GHOST
LANES = 128
EDGE = 8
PARTS = 8
SCALE = 0.8
MESH = pl.DeviceIdType.MESH
STAGES = (("core", "y"), ("x", "z"))
TRACER_STEP = 16
WEIGHTS_STEP = 112
DIAGONAL_STEP = 48
SCALED_STEP = 112
APPLY_STEP = 112
LAST_STEP = 160
FINAL_STEP = 80

GAIN = (-1.0, 1.0 / SCALE, 2.0 / SCALE, 2.0 / SCALE, 2.0 / SCALE)
SHIFT = (1.0, 0.0, 0.0, 0.0, 0.0)
BACK = (0.0, 0.0, SCALE / 2, SCALE / 2, SCALE / 2)
PAIRS = tuple((i, j) for j in range(ITERS + 1) for i in range(j + 1) if (i, j) != (ITERS, ITERS))


def roll(x, shift):
    return pltpu.roll(x, shift % x.shape[-1], x.ndim - 1)


def lane_of(shape):
    return lax.broadcasted_iota(jnp.int32, shape, len(shape) - 1)


def row_of(shape):
    return lax.broadcasted_iota(jnp.int32, shape, len(shape) - 2)


def extents(lon_count, lat_count):
    z = min(4, lon_count // 2)
    return {"core": 2, "z": z, "x": lon_count // (2 * z), "y": lat_count}


def stage_size(extent, axes):
    size = 1
    for axis in axes:
        size *= extent[axis]
    return size


def sweep(name, first, rows, step, body, start=0):
    whole = rows // step

    def chunk(i, carry):
        return body(pl.multiple_of(first + i * step, 8), step, carry)

    carry = lax.fori_loop(0, whole, chunk, start) if whole else start
    if rows % step:
        carry = body(first + whole * step, rows % step, carry)
    return carry


def remote(name, src, dst, sent, received, device):
    return pltpu.make_async_remote_copy(
        src, dst, sent, received, device_id=device, device_id_type=MESH)


def local_copy(name, src, dst, done):
    return pltpu.make_async_copy(src, dst, done)


def step(name, run):
    run()


def arrived(name, part, received):
    pltpu.make_async_copy(part, part, received).wait()


def face_flux(here, there, vel_here, vel_there, shared, level):
    carried = (vel_here + vel_there) * (here + there)
    return jnp.where(shared > level, 1.92 * (there - here) - carried, 0.0)


def ring_east(main, strip, lane):
    a, b = roll(main, -1), roll(strip, -1)
    last = lane == LANES - 1
    return jnp.where(last, b, a), jnp.where(last, a, b)


def ring_west(main, strip, lane):
    a, b = roll(main, 1), roll(strip, 1)
    first = lane == 0
    return jnp.where(first, b, a), jnp.where(first, a, b)


def solve(gram):
    size = ITERS + 1

    def product(left, right):
        total = None
        for i, a in enumerate(left):
            if a is None:
                continue
            inner = None
            for j, b in enumerate(right):
                if b is None:
                    continue
                term = gram[min(i, j), max(i, j)] * b
                inner = term if inner is None else inner + term
            total = a * inner if total is None else total + a * inner
        return total

    def operate(coeffs):
        out = [None] * size

        def add(k, value):
            out[k] = value if out[k] is None else out[k] + value

        for k in range(ITERS):
            if coeffs[k] is None:
                continue
            add(k + 1, coeffs[k] * (-1.0 / GAIN[k]))
            if SHIFT[k] != 1.0:
                add(k, coeffs[k] * (1.0 - SHIFT[k]))
            if BACK[k] != 0.0:
                add(k - 1, coeffs[k] * (-BACK[k]))
        return out

    one = jnp.ones_like(gram[0, 0])
    scaled = [one] + [None] * ITERS
    direction = list(scaled)
    surface = [None] * size
    rho = product(scaled, scaled)
    for turn in range(ITERS):
        image = operate(direction)
        step = rho / product(direction, image)
        for k in range(size):
            if direction[k] is not None:
                move = step * direction[k]
                surface[k] = move if surface[k] is None else surface[k] + move
            if image[k] is not None:
                move = step * image[k]
                scaled[k] = -move if scaled[k] is None else scaled[k] - move
        if turn == ITERS - 1:
            break
        rho_new = product(scaled, scaled)
        ratio = rho_new / rho
        direction = [
            s if d is None else s + ratio * d for s, d in zip(scaled, direction)
        ]
        rho = rho_new
    return surface[:ITERS], scaled


def kernel(
    lon_count, lat_count, rows,
    t_in, u_in, v_in, lev_in, forc_in, stor_in,
    new_out, surf_out, res_out,
    tr, ur, vr, li, fo, lv, st,
    beside_out, beside_w, beside_e, rows_out, rows_in,
    edge_out, edge_w, edge_e, edge_rows_out, edge_rows,
    flux, flux_sum, total, nt,
    w_e, w_n, w_ne, w_nw, w_er, w_ner, w_nwr, rdiag, diag, basis,
    surf, resid,
    in_sem, rows_send, rows_recv, beside_send, beside_recv, red_send, red_recv, out_sem, *boxes,
):
    lon, lat = lax.axis_index("lon"), lax.axis_index("lat")
    is_top = lat == lat_count - 1
    not_top = jnp.logical_not(is_top)
    not_bottom = lat > 0
    top = BASE + rows
    south = BASE - GHOST
    own = pl.ds(BASE, rows)
    inner = pl.ds(GHOST, rows)
    tile = (8, LANES)
    lane = lane_of(tile)
    row = row_of(tile)
    reach = rows + 2 * GHOST
    part = rows // PARTS

    def lanes(n):
        return lane_of((n, LANES))

    def row_is(r, n, which):
        return row_of((n, LANES)) + r == which

    east = lax.rem(lon + 1, lon_count)
    west = lax.rem(lon + lon_count - 1, lon_count)
    up_lat = jnp.where(is_top, lat, lat + 1)
    down_lat = jnp.maximum(lat - 1, 0)
    up_lon = jnp.where(is_top, lon_count - 1 - lon, lon)
    up_e = jnp.where(is_top, lax.rem(2 * lon_count - 2 - lon, lon_count), east)
    up_w = jnp.where(is_top, lax.rem(lon_count - lon, lon_count), west)
    self_e = jnp.logical_and(is_top, up_e == lon)
    self_w = jnp.logical_and(is_top, up_w == lon)
    other_e, other_w = jnp.logical_not(self_e), jnp.logical_not(self_w)

    extent = extents(lon_count, lat_count)
    here_at = {
        "core": lax.rem(lon, 2),
        "z": lax.rem(lon // 2, extent["z"]),
        "x": lon // (2 * extent["z"]),
        "y": lat,
    }

    def stage_peers(axes):
        place = 0
        for axis in axes:
            place = place * extent[axis] + here_at[axis]
        size = stage_size(extent, axes)
        peers = []
        for j in range(1, size):
            index = lax.rem(place + j, size)
            at = dict(here_at)
            rest = index
            for axis in reversed(axes):
                at[axis] = lax.rem(rest, extent[axis])
                rest = rest // extent[axis]
            device = {
                "lon": (at["x"] * extent["z"] + at["z"]) * 2 + at["core"], "lat": at["y"]}
            peers.append((index, device))
        return place, peers

    stages = [stage_peers(axes) for axes in STAGES]

    barrier = pltpu.get_barrier_semaphore()

    def greet(device):
        pl.semaphore_signal(barrier, inc=1, device_id=device, device_id_type=MESH)

    greet({"lon": east, "lat": lat})
    greet({"lon": west, "lat": lat})
    greet({"lon": up_lon, "lat": up_lat})

    @pl.when(other_e)
    def _():
        greet({"lon": up_e, "lat": up_lat})

    @pl.when(other_w)
    def _():
        greet({"lon": up_w, "lat": up_lat})

    @pl.when(not_bottom)
    def _():
        greet({"lon": lon, "lat": down_lat})
        greet({"lon": east, "lat": down_lat})
        greet({"lon": west, "lat": down_lat})

    loads = [
        local_copy("load", src, dst, in_sem.at[n]) for n, (src, dst) in enumerate((
            (lev_in, li), (stor_in, st.at[0, own, :]), (t_in, tr.at[:, inner, :]),
            (u_in, ur.at[:, inner, :]), (v_in, vr.at[:, inner, :]), (forc_in, fo),
        ))
    ]
    for load in loads:
        load.start()

    greeted = 3
    for _, peers in stages:
        for _, device in peers:
            greet(device)
        greeted += len(peers)
    greeted = greeted + jnp.where(self_e, 0, 1) + jnp.where(self_w, 0, 1) + jnp.where(not_bottom, 3, 0)

    nothing = jnp.zeros(tile, jnp.float32)
    for r in (south - 8, top + 8):
        at = pl.ds(r, 8)
        for half in range(2):
            for buffer in (lv, w_n, w_ne, w_nw):
                buffer[half, at, :] = nothing
            for k in range(ITERS + 1):
                basis[k, half, at, :] = nothing

    def fold(ranges):
        out = None
        for c, x in enumerate(ranges):
            moved = roll(x, EDGE + 16 * c)
            out = moved if out is None else jnp.where(lanes(part) // 16 == c, moved, out)
        return out

    def unfold(from_west, from_east):
        both = jnp.where(lanes(part) % 16 < EDGE, from_west, from_east)
        ends = jnp.logical_or(lanes(part) < EDGE, lanes(part) >= LANES - EDGE)
        return [
            jnp.where(ends, roll(both, -(EDGE + 16 * c)), 0.0) for c in range(PARTS)]

    def part_rows(c):
        return pl.ds(BASE + c * part, part)

    loads[0].wait()
    loads[1].wait()
    lv[0, own, :] = li[...].astype(jnp.float32)
    at_t, at_l, at_s = pl.ds(0, 2 * part), pl.ds(2 * part, part), pl.ds(3 * part, part)
    beside_out[at_l, :] = fold([lv[0, part_rows(c), :] for c in range(PARTS)])
    beside_out[at_s, :] = fold([st[0, part_rows(c), :] for c in range(PARTS)])
    edges = ((0, BASE, GHOST), (1, top - GHOST, GHOST + rows - 1))
    for side, r, _ in edges:
        rows_out[side, 0] = lv[0, pl.ds(r, GHOST), :]
        rows_out[side, 1] = st[0, pl.ds(r, GHOST), :]

    for load in loads[2:]:
        load.wait()

    def gather_ends(buffer, r, n):
        x = [buffer[k, pl.ds(r, n), :] for k in range(LEVELS)]
        lane = lanes(n)
        width = 2
        while len(x) > 1:
            window = jnp.logical_or(lane == 0, lane > LANES - width)
            x = [
                jnp.where(window, x[i + 1], roll(x[i], -width)) for i in range(0, len(x), 2)]
            width *= 2
        return x[0]

    def pack_ends(r, n, carry):
        out = None
        for c in range(PARTS // 2):
            for slot, buffer in enumerate((tr, ur)):
                moved = roll(gather_ends(buffer, GHOST + c * 2 * part + r, n), 32 * c + 16 * slot - 113)
                out = moved if out is None else jnp.where(
                    lanes(n) // 16 == 2 * c + slot, moved, out)
        beside_out[pl.ds(r, n), :] = out
        return carry

    sweep("ends", 0, 2 * part, part, pack_ends)
    for side, _, r in edges:
        for k in range(LEVELS):
            rows_out[side, 2, pl.ds(k, 1), :] = tr[k, pl.ds(r, 1), :]
            rows_out[side, 3, pl.ds(k, 1), :] = vr[k, pl.ds(r, 1), :]

    pl.semaphore_wait(barrier, greeted)

    def exchange(phase, beside_from, to_east, to_west, rows_from, rows_to, corners):
        def by_rows(slot, side, wide, place, to_lon, to_lat):
            src, dst = rows_from(side), rows_to.at[place]
            if not wide:
                src, dst = corners(src), corners(dst)
            return remote(
                "halo", src, dst, rows_send.at[phase, slot], rows_recv.at[phase, place],
                {"lon": to_lon, "lat": to_lat})

        go_e = remote(
            "halo", beside_from, to_east, beside_send.at[phase, 0], beside_recv.at[phase, 0],
            {"lon": east, "lat": lat})
        go_w = remote(
            "halo", beside_from, to_west, beside_send.at[phase, 1], beside_recv.at[phase, 1],
            {"lon": west, "lat": lat})
        go_up = by_rows(0, 1, True, jnp.where(is_top, 3, 0), up_lon, up_lat)
        go_up_e = by_rows(1, 1, False, jnp.where(is_top, 5, 1), up_e, up_lat)
        go_up_w = by_rows(2, 1, False, jnp.where(is_top, 4, 2), up_w, up_lat)
        go_down = by_rows(3, 0, True, 3, lon, down_lat)
        go_down_e = by_rows(4, 0, False, 4, east, down_lat)
        go_down_w = by_rows(5, 0, False, 5, west, down_lat)
        stay_e = local_copy(
            "halo", corners(rows_from(1)), corners(rows_to.at[5]), rows_recv.at[phase, 5])
        stay_w = local_copy(
            "halo", corners(rows_from(1)), corners(rows_to.at[4]), rows_recv.at[phase, 4])
        go_e.start()
        go_w.start()
        go_up.start()
        pl.when(other_e)(go_up_e.start)
        pl.when(other_w)(go_up_w.start)
        pl.when(self_e)(stay_e.start)
        pl.when(self_w)(stay_w.start)

        @pl.when(not_bottom)
        def _():
            go_down.start()
            go_down_e.start()
            go_down_w.start()

        def sent():
            go_e.wait_send()
            go_w.wait_send()
            go_up.wait_send()
            pl.when(other_e)(go_up_e.wait_send)
            pl.when(other_w)(go_up_w.wait_send)

            @pl.when(not_bottom)
            def _():
                go_down.wait_send()
                go_down_e.wait_send()
                go_down_w.wait_send()

        def received():
            arrived("halo", to_east, beside_recv.at[phase, 0])
            arrived("halo", to_west, beside_recv.at[phase, 1])
            arrived("halo", rows_to.at[3], rows_recv.at[phase, 3])
            arrived("halo", corners(rows_to.at[4]), rows_recv.at[phase, 4])
            arrived("halo", corners(rows_to.at[5]), rows_recv.at[phase, 5])

            @pl.when(not_bottom)
            def _():
                arrived("halo", rows_to.at[0], rows_recv.at[phase, 0])
                arrived("halo", corners(rows_to.at[1]), rows_recv.at[phase, 1])
                arrived("halo", corners(rows_to.at[2]), rows_recv.at[phase, 2])

        return sent, received

    first_sent, first_received = exchange(
        0, beside_out, beside_w, beside_e, lambda side: rows_out.at[side], rows_in,
        lambda ref: ref.at[pl.ds(0, 2)])

    def tracer_rows(r, n, carry):
        at, up, down = pl.ds(r, n), pl.ds(r + 1, n), pl.ds(r - 1, n)
        wide, wide_up, wide_down = (pl.ds(r + GHOST + d, n) for d in (0, 1, -1))
        depth = lv[0, wide, :]
        open_e = jnp.where(
            lanes(n) == LANES - 1, 0.0, jnp.minimum(depth, roll(depth, -1)))
        open_n = jnp.where(
            row_is(r, n, GHOST + rows - 1), 0.0, jnp.minimum(depth, lv[0, wide_up, :]))
        open_s = jnp.where(
            row_is(r, n, GHOST), 0.0, jnp.minimum(depth, lv[0, wide_down, :]))
        below = None
        summed = None
        here = tr[0, at, :]
        for k in range(LEVELS):
            vel = vr[k, at, :]
            zonal = ur[k, at, :]
            flux_e = face_flux(here, roll(here, -1), zonal, roll(zonal, -1), open_e, k)
            flux_n = face_flux(here, tr[k, up, :], vel, vr[k, up, :], open_n, k)
            flux_s = face_flux(tr[k, down, :], here, vr[k, down, :], vel, open_s, k)
            change = 0.0625 * ((flux_e - roll(flux_e, 1)) + (flux_n - flux_s))
            result = here + change
            if below is not None:
                result = result - below
            if k + 1 < LEVELS:
                above = tr[k + 1, at, :]
                below = jnp.where(depth > k + 1, 0.1 * (above - here), 0.0)
                result = result + below
                here = above
            nt[k, pl.ds(r - GHOST, n), :] = result
            wet_part = jnp.where(depth > k, result, 0.0)
            summed = wet_part if summed is None else summed + wet_part
        total[pl.ds(r - GHOST, n), :] = summed
        return carry

    sweep("tracer", GHOST, rows, TRACER_STEP, tracer_rows)

    first_received()

    def clear(buffer):
        for place in range(3):
            buffer[place] = jnp.zeros(buffer.shape[1:], buffer.dtype)

    pl.when(jnp.logical_not(not_bottom))(lambda: clear(rows_in))

    def swap(x, bit, axis):
        size = x.shape[axis]
        index = lax.broadcasted_iota(jnp.int32, x.shape, axis)
        low = (index // bit) % 2 == 0
        return jnp.where(low, pltpu.roll(x, size - bit, axis), pltpu.roll(x, bit, axis))

    def mirror_lanes(x):
        for bit in (1, 2, 4, 8, 16, 32, 64):
            x = swap(x, bit, 1)
        return x

    def mirror(x):
        x = mirror_lanes(x)
        for bit in (1, 2, 4):
            x = swap(x, bit, 0)
        return x

    @pl.when(is_top)
    def _():
        for place in (3, 4, 5):
            for field in range(2):
                rows_in[place, field] = mirror(rows_in[place, field])
        rows_in[3, 2] = mirror_lanes(rows_in[3, 2])

    level_row = row.astype(jnp.float32)
    carry_north = jnp.where(is_top, 0.0, 1.0)
    own_first, own_last = rows_out[0], rows_out[1]
    shared_n = jnp.minimum(own_last[0][7:8], rows_in[3, 0][0:1])
    flux_n = jnp.where(
        shared_n > level_row,
        0.0625 * (1.92 * (rows_in[3, 2] - own_last[2])
                  - carry_north * (own_last[3] + rows_in[3, 3]) * (own_last[2] + rows_in[3, 2])),
        0.0)
    shared_s = jnp.minimum(own_first[0][0:1], rows_in[0, 0][7:8])
    flux_s = jnp.where(
        shared_s > level_row,
        0.0625 * (1.92 * (own_first[2] - rows_in[0, 2])
                  - (own_first[3] + rows_in[0, 3]) * (own_first[2] + rows_in[0, 2])),
        0.0)
    first_own, last_own = pl.ds(0, 8), pl.ds(rows - 8, 8)
    for k in range(LEVELS):
        nt[k, last_own, :] = nt[k, last_own, :] + jnp.where(row == 7, flux_n[k:k + 1], 0.0)
        nt[k, first_own, :] = nt[k, first_own, :] - jnp.where(row == 0, flux_s[k:k + 1], 0.0)
    total[last_own, :] = total[last_own, :] + jnp.where(
        row == 7, jnp.sum(flux_n, axis=0, keepdims=True), 0.0)
    total[first_own, :] = total[first_own, :] - jnp.where(
        row == 0, jnp.sum(flux_s, axis=0, keepdims=True), 0.0)

    depths = [buffer[at_l, :] for buffer in (beside_out, beside_w, beside_e)]
    for half in range(2):
        at = pl.ds(half * part, part)
        lane_p = lanes(part)
        even = lane_p % 2 == 0
        mine, from_w, from_e = beside_out[at, :], beside_w[at, :], beside_e[at, :]
        here = jnp.where(even, mine, roll(from_w, 1))
        there = jnp.where(even, roll(from_e, -1), mine)
        carried = roll(here + there, -16) * (here + there)
        d_mine, d_w, d_e = depths
        shared = jnp.where(
            lane_p % 16 == 7, jnp.minimum(d_mine, roll(d_e, -1)),
            jnp.where(lane_p % 16 == 8, jnp.minimum(roll(d_w, 1), d_mine), 0.0))
        shared = jnp.where((lane_p // 16) % 2 == half, shared, 0.0)
        shared = roll(shared, -7 - 16 * half)
        for shift in (2, 4, 8):
            shared = shared + roll(shared, shift)
        level = ((lane_p % 16) // 2).astype(jnp.float32)
        through = jnp.where(
            jnp.logical_and(shared > level, lane_p % 32 < 16),
            0.0625 * (1.92 * (there - here) - carried), 0.0)
        through = jnp.where(even, through, -through)
        flux[at, :] = through
        for shift in (2, 4, 8):
            through = through + roll(through, -shift)
        flux_sum[at, :] = through

    def right_side(c):
        at = pl.ds(c * part, part)
        lane_p = lanes(part)
        ends = jnp.logical_or(lane_p == 0, lane_p == LANES - 1)
        across = roll(flux_sum[pl.ds((c % 2) * part, part), :], 127 - 32 * (c // 2))
        summed = total[at, :] + jnp.where(ends, across, 0.0)
        value = jnp.where(lv[0, part_rows(c), :] > 0.0, fo[at, :], 0.0) + summed * 8.0 ** -0.5
        basis[0, 0, part_rows(c), :] = value
        return value

    edge_out[...] = fold([right_side(c) for c in range(PARTS)])
    for side, r, _ in edges:
        edge_rows_out[side] = basis[0, 0, pl.ds(r, GHOST), :]
    second_sent, second_received = exchange(
        1, edge_out, edge_w, edge_e, lambda side: edge_rows_out.at[side], edge_rows,
        lambda ref: ref)

    def place_rows(buffer, get):
        for r, across, w_at, e_at in ((south, 0, 1, 2), (top, 3, 4, 5)):
            at = pl.ds(r, GHOST)
            buffer[0, at, :] = get(across)
            buffer[1, at, :] = jnp.where(
                lane < EDGE, get(e_at), jnp.where(lane >= LANES - EDGE, get(w_at), 0.0))

    for buffer, at, field in ((lv, at_l, 0), (st, at_s, 1)):
        for c, x in enumerate(unfold(beside_w[at, :], beside_e[at, :])):
            buffer[1, part_rows(c), :] = x
        place_rows(buffer, lambda place, field=field: rows_in[place, field])

    fold_row = jnp.where(is_top, top - 1, -1)

    def weigh(a, b):
        return a * b / (a + b + 1.0)

    def weights_rows(r, n, carry):
        at, up = pl.ds(r, n), pl.ds(r + 1, n)
        lane = lanes(n)
        d_m, d_s = lv[0, at, :], lv[1, at, :]
        n_m, n_s = lv[0, up, :], lv[1, up, :]
        e_m, e_s = ring_east(d_m, d_s, lane)
        ne_m, ne_s = ring_east(n_m, n_s, lane)
        nw_m, nw_s = ring_west(n_m, n_s, lane)
        corner = jnp.where(row_is(r, n, fold_row), 0.0, 0.25)
        east_m, east_s = weigh(d_m, e_m), weigh(d_s, e_s)
        neast_m, neast_s = corner * weigh(d_m, ne_m), corner * weigh(d_s, ne_s)
        nwest_m, nwest_s = corner * weigh(d_m, nw_m), corner * weigh(d_s, nw_s)
        w_e[0, at, :], w_e[1, at, :] = east_m, east_s
        w_n[0, at, :], w_n[1, at, :] = weigh(d_m, n_m), weigh(d_s, n_s)
        w_ne[0, at, :], w_ne[1, at, :] = neast_m, neast_s
        w_nw[0, at, :], w_nw[1, at, :] = nwest_m, nwest_s
        w_er[0, at, :], w_er[1, at, :] = ring_west(east_m, east_s, lane)
        w_ner[0, at, :], w_ner[1, at, :] = ring_west(neast_m, neast_s, lane)
        w_nwr[0, at, :], w_nwr[1, at, :] = ring_east(nwest_m, nwest_s, lane)
        return carry

    sweep("weights", south, reach, WEIGHTS_STEP, weights_rows)

    def diagonal_rows(r, n, carry):
        at, down = pl.ds(r, n), pl.ds(r - 1, n)
        for half in range(2):
            whole = (
                st[half, at, :] + w_e[half, at, :] + w_er[half, at, :] + w_n[half, at, :]
                + w_n[half, down, :] + w_ne[half, at, :] + w_nw[half, at, :]
                + w_ner[half, down, :] + w_nwr[half, down, :])
            rdiag[half, at, :] = jnp.where(whole > 0.0, 1.0 / whole, 0.0)
            if half == 0:
                diag[at, :] = whole
        return carry

    sweep("diagonal", south, reach, DIAGONAL_STEP, diagonal_rows)
    diag[pl.ds(south, GHOST), :] = nothing
    diag[pl.ds(top, GHOST), :] = nothing

    def ends_rows(r, n, carry):
        lane = lanes(n)
        ends = jnp.logical_or(lane == 0, lane == LANES - 1)
        across = flux[pl.ds(r, n), :]
        for c in range(PARTS // 2):
            at = pl.ds(c * 2 * part + r, n)
            for k in range(LEVELS):
                nt[k, at, :] = nt[k, at, :] + jnp.where(
                    ends, roll(across, 127 - 32 * c - 2 * k), 0.0)
        return carry

    sweep("new", 0, 2 * part, part, ends_rows)
    out_new = local_copy("out", nt, new_out, out_sem.at[0])
    out_new.start()

    second_received()
    pl.when(jnp.logical_not(not_bottom))(lambda: clear(edge_rows))

    @pl.when(is_top)
    def _():
        for place in (3, 4, 5):
            edge_rows[place] = mirror(edge_rows[place])

    for c, x in enumerate(unfold(edge_w[...], edge_e[...])):
        basis[0, 1, part_rows(c), :] = x
    place_rows(basis.at[0], lambda place: edge_rows[place])

    gram = {}

    def fold_rows(x):
        return jnp.sum(x.reshape(x.shape[0] // 8, 8, LANES), axis=0)

    def scaled_rows(r, n, acc):
        at = pl.ds(r, n)
        for half in range(2):
            x = basis[0, half, at, :]
            y = x * rdiag[half, at, :]
            basis[0, half, at, :] = y
            if half == 0:
                acc = acc + fold_rows(diag[at, :] * y * y)
        return acc

    gram[0, 0] = sweep("scaled", south, reach, SCALED_STEP, scaled_rows, nothing)

    def neighbours_sum(k, r, n, halves):
        at, up, down = pl.ds(r, n), pl.ds(r + 1, n), pl.ds(r - 1, n)
        lane = lanes(n)
        sums, to_west, to_east = [], [], []
        for half in range(2):
            x = basis[k, half, at, :]
            x_n = basis[k, half, up, :]
            x_s = basis[k, half, down, :]
            to_east.append(
                w_e[half, at, :] * x + w_ne[half, down, :] * x_s + w_nwr[half, at, :] * x_n)
            to_west.append(
                w_er[half, at, :] * x + w_nw[half, down, :] * x_s + w_ner[half, at, :] * x_n)
            if half < halves:
                sums.append(w_n[half, at, :] * x_n + w_n[half, down, :] * x_s)
        from_west = ring_west(to_east[0], to_east[1], lane)
        from_east = ring_east(to_west[0], to_west[1], lane)
        return [sums[h] + from_west[h] + from_east[h] for h in range(halves)]

    def apply_rows(k, r, n, halves):
        at = pl.ds(r, n)
        sums = neighbours_sum(k, r, n, halves)
        out = []
        for half in range(halves):
            x = basis[k, half, at, :]
            y = rdiag[half, at, :] * sums[half]
            if SHIFT[k] != 0.0:
                y = y - SHIFT[k] * x
            if BACK[k] != 0.0:
                y = y - BACK[k] * basis[k - 1, half, at, :]
            y = GAIN[k] * y
            basis[k + 1, half, at, :] = y
            out.append(y)
        return out[0]

    for k in range(ITERS):
        last = k == ITERS - 1
        terms = [p for p in PAIRS if p[1] == k + 1]

        def apply_own(r, n, accs, k=k, terms=terms, halves=1 if last else 2):
            at = pl.ds(r, n)
            y = apply_rows(k, r, n, halves)
            scaled = diag[at, :] * y
            return tuple(
                acc + fold_rows(scaled * (y if a == k + 1 else basis[a, 0, at, :]))
                for acc, (a, _) in zip(accs, terms))

        sums = sweep(
            "apply", BASE if last else south, rows if last else reach,
            LAST_STEP if last else APPLY_STEP, apply_own, tuple(nothing for _ in terms))
        for p, s in zip(terms, sums):
            gram[p] = s

    per_lane = [jnp.sum(gram[p], axis=0, keepdims=True) for p in PAIRS]
    per_lane = per_lane + [jnp.zeros((1, LANES), jnp.float32)] * (24 - len(per_lane))
    stacked = jnp.sum(jnp.concatenate(per_lane, axis=0), axis=1, keepdims=True)
    count = stacked.shape[0]
    own_lane = lane_of((count, LANES)) == row_of((count, LANES))
    summed = jnp.sum(jnp.where(own_lane, stacked, 0.0), axis=0, keepdims=True)

    sends = []
    for stage, (place, peers) in enumerate(stages):
        box = boxes[stage]
        box[pl.ds(place, 1), :, :] = summed[None]
        for n, (_, device) in enumerate(peers):
            copy = remote(
                "red", box.at[place], box.at[place],
                red_send.at[stage, n], red_recv.at[stage, place], device)
            copy.start()
            sends.append(copy)
        for index, _ in peers:
            arrived("red", box.at[index], red_recv.at[stage, index])
        summed = box[0]
        for n in range(1, len(peers) + 1):
            summed = summed + box[n]

    spread = jnp.sum(
        jnp.where(own_lane, jnp.broadcast_to(summed, (count, LANES)), 0.0),
        axis=1, keepdims=True)
    sums = {
        p: jnp.broadcast_to(spread[n:n + 1], tile) for n, p in enumerate(PAIRS)
    }
    surface_by, scaled_by = solve(sums)

    surface_by = [c[0:1] for c in surface_by]
    scaled_by = [c[0:1] for c in scaled_by]

    def final_rows(r, n, carry):
        at = pl.ds(r, n)
        to = pl.ds(pl.multiple_of(r - BASE, 8), n)
        x = [basis[k, 0, at, :] for k in range(ITERS + 1)]
        level_at = surface_by[0] * x[0]
        left = scaled_by[0] * x[0]
        for k in range(1, ITERS + 1):
            if k < ITERS:
                level_at = level_at + surface_by[k] * x[k]
            left = left + scaled_by[k] * x[k]
        surf[to, :] = level_at
        resid[to, :] = diag[at, :] * left
        return carry

    sweep("final", BASE, rows, FINAL_STEP, final_rows)
    out_surf = local_copy("out", surf, surf_out, out_sem.at[1])
    out_res = local_copy("out", resid, res_out, out_sem.at[2])
    out_surf.start()
    out_res.start()

    first_sent()
    second_sent()
    for copy in sends:
        copy.wait_send()
    out_new.wait()
    out_surf.wait()
    out_res.wait()


def local(lon_count, lat_count, tracer, east_vel, north_vel, levels, forcing, storage):
    rows = tracer.shape[1]
    flat = (rows + 4 * GHOST, LANES)
    part = rows // PARTS
    f32 = jnp.float32
    extent = extents(lon_count, lat_count)
    sizes = [stage_size(extent, axes) for axes in STAGES]

    def vmem(*shape, dtype=f32):
        return pltpu.VMEM(shape, dtype)

    cube = vmem(LEVELS, rows + 2 * GHOST, LANES)
    pair = vmem(2, *flat)
    block = vmem(rows, LANES)
    beside = vmem(4 * part, LANES)
    edge = vmem(part, LANES)
    dma = pltpu.SemaphoreType.DMA
    anywhere = pl.BlockSpec(memory_space=pl.ANY)
    outs = (
        jax.ShapeDtypeStruct(tracer.shape, f32),
        jax.ShapeDtypeStruct(levels.shape, f32),
        jax.ShapeDtypeStruct(levels.shape, f32),
    )
    return pl.pallas_call(
        functools.partial(kernel, lon_count, lat_count, rows),
        out_shape=outs,
        in_specs=[anywhere] * 6,
        out_specs=(anywhere,) * 3,
        scratch_shapes=[
            cube, cube, cube, vmem(rows, LANES, dtype=jnp.int32), block, pair, pair,
            beside, beside, beside, vmem(2, 4, 8, LANES), vmem(6, 4, 8, LANES),
            edge, edge, edge, vmem(2, 8, LANES), vmem(6, 8, LANES),
            vmem(2 * part, LANES), vmem(2 * part, LANES), block, vmem(LEVELS, rows, LANES),
            pair, pair, pair, pair, pair, pair, pair, pair, vmem(*flat),
            vmem(ITERS + 1, 2, *flat),
            block, block,
            dma((6,)), dma((2, 6)), dma((2, 6)), dma((2, 2)), dma((2, 2)),
            dma((len(sizes), max(sizes))), dma((len(sizes), max(sizes))), dma((3,)),
            *[vmem(size, 1, LANES) for size in sizes],
        ],
        compiler_params=pltpu.CompilerParams(
            collective_id=0, has_side_effects=True, vmem_limit_bytes=61 * 2**20
        ),
        cost_estimate=pl.CostEstimate(flops=10**8, bytes_accessed=6 * 10**6, transcendentals=0),
        name="ocean_step",
    )(tracer, east_vel, north_vel, levels, forcing, storage)


def solution(mesh):
    cube, flat = P(None, "lat", "lon"), P("lat", "lon")
    return jax.shard_map(
        functools.partial(local, mesh.shape["lon"], mesh.shape["lat"]),
        mesh=mesh,
        in_specs=(cube, cube, cube, flat, flat, flat),
        out_specs=(cube, flat, flat),
        check_vma=False,
    )
```

time: 45.8 us -> 36.9 us (0.81)
  Pallas kernels: 41 us -> 32.3 us
    pallas_call x1, Pallas kernels: 41 us -> 32.3 us  [local(): pl.pallas_call(functools.partial(kernel, lon_count, lat_count, rows), out...]
where the time goes in v3:
time: 36.9 us; the launch traced here: 36.8 us
  Pallas kernels  32.3 us (88%)
  local copies, waits for them, and re-layouts  3.85 us (10%)
  between operations  0.66 us (2%)
    pallas_call x1, Pallas kernels, local(): pl.pallas_call(functools.partial(kernel, lon_count, lat_count, rows), out...  32.3 us
    unnamed x7, local copies, waits for them, and re-layouts  3.85 us

profile of v3, /device:TPU:0, one launch (start us, length us, event | category | flops | bytes accessed | tf_op | source)
XLA Modules:
  0.0 36.8 jit_solution(17719511038406378500)
XLA Ops:
  0.6 32.3 %ocean_step.1 = (f32[8,320,128]{2,1,0:T(8,128)}, f32[320,128]{1,0:T(8,128)}, f32[320,128]{1,0:T(8,128)}) custom-call(f32[8,320,128]{2,1,0:T(8,128)} %t_in.1, f32[8,320,128]{2,1,0:T(8,128)} %u_in.1, f32[8,320,128]{2,1,0:T(8,128)} %v_in.1, s32[320,128]{1,0:T(8,128)} %lev_in.1, f32[320,128]{1,0:T(8,128)} %forc_in.1, f32[320,128]{1,0:T(8,128)} %stor_in.1), custom_call_target="tpu_custom_call" | custom-call | flops 100000000 | bytes 6000000 | tf_op jit(solution)/shard_map/ocean_step/pallas_call | solution.py:786
  32.9 0.0 copy-start.1
  32.9 0.0 copy-start
  32.9 2.5 %copy.12 = f32[8,320,128]{2,1,0:T(8,128)} copy(f32[8,320,128]{2,1,0:T(8,128)} %get-tuple-element.6) | data formatting | bytes 2621440
  35.5 0.0 copy-done.1
  35.5 0.7 %copy.13 = f32[320,128]{1,0:T(8,128)} copy(f32[320,128]{1,0:T(8,128)S(1)} %copy-done.1) | data formatting | bytes 327680
  36.1 0.0 copy-done
  36.1 0.7 %copy.14 = f32[320,128]{1,0:T(8,128)} copy(f32[320,128]{1,0:T(8,128)S(1)} %copy-done) | data formatting | bytes 327680
Async XLA Ops:
  32.9 2.5 %copy-start.1 = (f32[320,128]{1,0:T(8,128)S(1)}, f32[320,128]{1,0:T(8,128)}, u32[]{:S(2)}) copy-start(f32[320,128]{1,0:T(8,128)} %get-tuple-element.7) | copy-start | bytes 491524
  32.9 3.2 %copy-start = (f32[320,128]{1,0:T(8,128)S(1)}, f32[320,128]{1,0:T(8,128)}, u32[]{:S(2)}) copy-start(f32[320,128]{1,0:T(8,128)} %get-tuple-element.8) | copy-start | bytes 491524

commit v4 on v3

--- a/solution.py
+++ b/solution.py
@@ -1,4 +1,5 @@
 import functools
+import itertools
 
 import jax
 import jax.numpy as jnp
@@ -212,21 +213,24 @@
     }
 
     def stage_peers(axes):
-        place = 0
-        for axis in axes:
-            place = place * extent[axis] + here_at[axis]
-        size = stage_size(extent, axes)
+        def index_of(at):
+            index = 0
+            for axis in axes:
+                index = index * extent[axis] + at[axis]
+            return index
+
+        moves = sorted(
+            itertools.product(*(range(extent[axis]) for axis in axes)),
+            key=lambda move: -sum(min(d, extent[a] - d) for d, a in zip(move, axes)))
         peers = []
-        for j in range(1, size):
-            index = lax.rem(place + j, size)
+        for move in moves[:-1]:
             at = dict(here_at)
-            rest = index
-            for axis in reversed(axes):
-                at[axis] = lax.rem(rest, extent[axis])
-                rest = rest // extent[axis]
+            for axis, d in zip(axes, move):
+                at[axis] = lax.rem(here_at[axis] + d, extent[axis])
             device = {
                 "lon": (at["x"] * extent["z"] + at["z"]) * 2 + at["core"], "lat": at["y"]}
-            peers.append((index, device))
+            peers.append((index_of(at), device))
+        place = index_of(here_at)
         return place, peers
 
     stages = [stage_peers(axes) for axes in STAGES]
@@ -760,6 +764,20 @@
     out_res.wait()
 
 
+def hand_over(new, surf, res, new_out, surf_out, res_out, cube, flat, in_sem, out_sem):
+    pieces = [(surf, flat.at[0], surf_out), (res, flat.at[1], res_out)] + [
+        (new.at[k], cube.at[k], new_out.at[k]) for k in range(LEVELS)]
+    reads = [pltpu.make_async_copy(a, b, in_sem.at[n]) for n, (a, b, _) in enumerate(pieces)]
+    writes = [pltpu.make_async_copy(b, c, out_sem.at[n]) for n, (_, b, c) in enumerate(pieces)]
+    for read in reads:
+        read.start()
+    for read, write in zip(reads, writes):
+        read.wait()
+        write.start()
+    for write in writes:
+        write.wait()
+
+
 def local(lon_count, lat_count, tracer, east_vel, north_vel, levels, forcing, storage):
     rows = tracer.shape[1]
     flat = (rows + 4 * GHOST, LANES)
@@ -783,7 +801,7 @@
         jax.ShapeDtypeStruct(levels.shape, f32),
         jax.ShapeDtypeStruct(levels.shape, f32),
     )
-    return pl.pallas_call(
+    results = pl.pallas_call(
         functools.partial(kernel, lon_count, lat_count, rows),
         out_shape=outs,
         in_specs=[anywhere] * 6,
@@ -806,6 +824,18 @@
         cost_estimate=pl.CostEstimate(flops=10**8, bytes_accessed=6 * 10**6, transcendentals=0),
         name="ocean_step",
     )(tracer, east_vel, north_vel, levels, forcing, storage)
+    return pl.pallas_call(
+        hand_over,
+        out_shape=outs,
+        in_specs=[anywhere] * 3,
+        out_specs=(anywhere,) * 3,
+        scratch_shapes=[
+            vmem(*tracer.shape), vmem(2, rows, LANES),
+            dma((LEVELS + 2,)), dma((LEVELS + 2,)),
+        ],
+        compiler_params=pltpu.CompilerParams(vmem_limit_bytes=61 * 2**20),
+        name="hand_over",
+    )(*results)
 
 
 def solution(mesh):

time: 36.9 us -> 35.3 us (0.957)
  local copies, waits for them, and re-layouts: 3.85 us -> 0 us
  Pallas kernels: 32.3 us -> 34.5 us
    unnamed x7 -> x0, local copies, waits for them, and re-layouts: 3.85 us -> none
    pallas_call x0 -> x1, Pallas kernels: none -> 2.35 us  [local(): pl.pallas_call(hand_over, out_shape=outs, in_specs=[anywhere] * 3, out_sp...]
where the time goes in v4:
time: 35.3 us; the launch traced here: 35.1 us
  Pallas kernels  34.5 us (98%)
  between operations  0.64 us (2%)
    pallas_call x1, Pallas kernels, local(): pl.pallas_call(functools.partial(kernel, lon_count, lat_count, rows), out...  32.2 us
    pallas_call x1, Pallas kernels, local(): pl.pallas_call(hand_over, out_shape=outs, in_specs=[anywhere] * 3, out_sp...  2.35 us

profile of v4, /device:TPU:0, one launch (start us, length us, event | category | flops | bytes accessed | tf_op | source)
XLA Modules:
  0.0 35.1 jit_solution(4042086895971828802)
XLA Ops:
  0.6 32.2 %ocean_step.1 = (f32[8,320,128]{2,1,0:T(8,128)}, f32[320,128]{1,0:T(8,128)}, f32[320,128]{1,0:T(8,128)}) custom-call(f32[8,320,128]{2,1,0:T(8,128)} %t_in.1, f32[8,320,128]{2,1,0:T(8,128)} %u_in.1, f32[8,320,128]{2,1,0:T(8,128)} %v_in.1, s32[320,128]{1,0:T(8,128)} %lev_in.1, f32[320,128]{1,0:T(8,128)} %forc_in.1, f32[320,128]{1,0:T(8,128)} %stor_in.1), custom_call_target="tpu_custom_call" | custom-call | flops 100000000 | bytes 6000000 | tf_op jit(solution)/shard_map/ocean_step/pallas_call | solution.py:804
  32.8 2.3 %hand_over.1 = (f32[8,320,128]{2,1,0:T(8,128)}, f32[320,128]{1,0:T(8,128)}, f32[320,128]{1,0:T(8,128)}) custom-call(f32[8,320,128]{2,1,0:T(8,128)} %get-tuple-element.6.new, f32[320,128]{1,0:T(8,128)} %get-tuple-element.7.surf, f32[320,128]{1,0:T(8,128)} %get-tuple-element.8.res), custom_call_target="tpu_custom_call" | custom-call | tf_op jit(solution)/shard_map/hand_over/pallas_call | solution.py:827

commit v5 on v4

--- a/solution.py
+++ b/solution.py
@@ -167,6 +167,7 @@
     new_out, surf_out, res_out,
     tr, ur, vr, li, fo, lv, st,
     beside_out, beside_w, beside_e, rows_out, rows_in,
+    ends_out, ends_w, ends_e, vel_out, vel_send, vel_in, folded_out,
     edge_out, edge_w, edge_e, edge_rows_out, edge_rows,
     flux, flux_sum, total, nt,
     w_e, w_n, w_ne, w_nw, w_er, w_ner, w_nwr, rdiag, diag, basis,
@@ -193,6 +194,15 @@
     def row_is(r, n, which):
         return row_of((n, LANES)) + r == which
 
+    loads = [
+        local_copy("load", src, dst, in_sem.at[n]) for n, (src, dst) in enumerate((
+            (lev_in, li), (stor_in, st.at[0, own, :]), (t_in, tr.at[:, inner, :]),
+            (u_in, ur.at[:, inner, :]), (v_in, vr.at[:, inner, :]), (forc_in, fo),
+        ))
+    ]
+    for load in loads:
+        load.start()
+
     east = lax.rem(lon + 1, lon_count)
     west = lax.rem(lon + lon_count - 1, lon_count)
     up_lat = jnp.where(is_top, lat, lat + 1)
@@ -258,15 +268,6 @@
         greet({"lon": east, "lat": down_lat})
         greet({"lon": west, "lat": down_lat})
 
-    loads = [
-        local_copy("load", src, dst, in_sem.at[n]) for n, (src, dst) in enumerate((
-            (lev_in, li), (stor_in, st.at[0, own, :]), (t_in, tr.at[:, inner, :]),
-            (u_in, ur.at[:, inner, :]), (v_in, vr.at[:, inner, :]), (forc_in, fo),
-        ))
-    ]
-    for load in loads:
-        load.start()
-
     greeted = 3
     for _, peers in stages:
         for _, device in peers:
@@ -274,15 +275,6 @@
         greeted += len(peers)
     greeted = greeted + jnp.where(self_e, 0, 1) + jnp.where(self_w, 0, 1) + jnp.where(not_bottom, 3, 0)
 
-    nothing = jnp.zeros(tile, jnp.float32)
-    for r in (south - 8, top + 8):
-        at = pl.ds(r, 8)
-        for half in range(2):
-            for buffer in (lv, w_n, w_ne, w_nw):
-                buffer[half, at, :] = nothing
-            for k in range(ITERS + 1):
-                basis[k, half, at, :] = nothing
-
     def fold(ranges):
         out = None
         for c, x in enumerate(ranges):
@@ -302,7 +294,7 @@
     loads[0].wait()
     loads[1].wait()
     lv[0, own, :] = li[...].astype(jnp.float32)
-    at_t, at_l, at_s = pl.ds(0, 2 * part), pl.ds(2 * part, part), pl.ds(3 * part, part)
+    at_l, at_s = pl.ds(0, part), pl.ds(part, part)
     beside_out[at_l, :] = fold([lv[0, part_rows(c), :] for c in range(PARTS)])
     beside_out[at_s, :] = fold([st[0, part_rows(c), :] for c in range(PARTS)])
     edges = ((0, BASE, GHOST), (1, top - GHOST, GHOST + rows - 1))
@@ -310,8 +302,76 @@
         rows_out[side, 0] = lv[0, pl.ds(r, GHOST), :]
         rows_out[side, 1] = st[0, pl.ds(r, GHOST), :]
 
-    for load in loads[2:]:
-        load.wait()
+    def exchange(phase, beside_from, to_east, to_west, rows_from, rows_to, corners, before=None):
+        def by_rows(slot, side, place, to_lon, to_lat):
+            return remote(
+                "halo", rows_from.at[side], rows_to.at[place],
+                rows_send.at[phase, slot], rows_recv.at[phase, place],
+                {"lon": to_lon, "lat": to_lat})
+
+        go_e = remote(
+            "halo", beside_from, to_east, beside_send.at[phase, 0], beside_recv.at[phase, 0],
+            {"lon": east, "lat": lat})
+        go_w = remote(
+            "halo", beside_from, to_west, beside_send.at[phase, 1], beside_recv.at[phase, 1],
+            {"lon": west, "lat": lat})
+        go_up = by_rows(0, 1, jnp.where(is_top, 3, 0), up_lon, up_lat)
+        go_down = by_rows(3, 0, 3, lon, down_lat)
+        if corners:
+            go_up_e = by_rows(1, 1, jnp.where(is_top, 5, 1), up_e, up_lat)
+            go_up_w = by_rows(2, 1, jnp.where(is_top, 4, 2), up_w, up_lat)
+            go_down_e = by_rows(4, 0, 4, east, down_lat)
+            go_down_w = by_rows(5, 0, 5, west, down_lat)
+            stay_e = local_copy(
+                "halo", rows_from.at[1], rows_to.at[5], rows_recv.at[phase, 5])
+            stay_w = local_copy(
+                "halo", rows_from.at[1], rows_to.at[4], rows_recv.at[phase, 4])
+        go_e.start()
+        go_w.start()
+        if before is not None:
+            before()
+        if corners:
+            pl.when(other_e)(go_up_e.start)
+            pl.when(other_w)(go_up_w.start)
+            pl.when(self_e)(stay_e.start)
+            pl.when(self_w)(stay_w.start)
+
+            @pl.when(not_bottom)
+            def _():
+                go_down_e.start()
+                go_down_w.start()
+        go_up.start()
+        pl.when(not_bottom)(go_down.start)
+
+        def sent():
+            go_e.wait_send()
+            go_w.wait_send()
+            go_up.wait_send()
+            pl.when(not_bottom)(go_down.wait_send)
+            if corners:
+                pl.when(other_e)(go_up_e.wait_send)
+                pl.when(other_w)(go_up_w.wait_send)
+
+                @pl.when(not_bottom)
+                def _():
+                    go_down_e.wait_send()
+                    go_down_w.wait_send()
+
+        def received():
+            arrived("halo", to_east, beside_recv.at[phase, 0])
+            arrived("halo", to_west, beside_recv.at[phase, 1])
+            for place in (3, 4, 5) if corners else (3,):
+                arrived("halo", rows_to.at[place], rows_recv.at[phase, place])
+
+            @pl.when(not_bottom)
+            def _():
+                for place in (0, 1, 2) if corners else (0,):
+                    arrived("halo", rows_to.at[place], rows_recv.at[phase, place])
+
+        return sent, received
+
+    loads[2].wait()
+    loads[3].wait()
 
     def gather_ends(buffer, r, n):
         x = [buffer[k, pl.ds(r, n), :] for k in range(LEVELS)]
@@ -331,87 +391,61 @@
                 moved = roll(gather_ends(buffer, GHOST + c * 2 * part + r, n), 32 * c + 16 * slot - 113)
                 out = moved if out is None else jnp.where(
                     lanes(n) // 16 == 2 * c + slot, moved, out)
-        beside_out[pl.ds(r, n), :] = out
+        ends_out[pl.ds(r, n), :] = out
         return carry
 
     sweep("ends", 0, 2 * part, part, pack_ends)
-    for side, _, r in edges:
-        for k in range(LEVELS):
-            rows_out[side, 2, pl.ds(k, 1), :] = tr[k, pl.ds(r, 1), :]
-            rows_out[side, 3, pl.ds(k, 1), :] = vr[k, pl.ds(r, 1), :]
+    def swap(x, bit, bits, axis):
+        size = x.shape[axis]
+        index = (lax.broadcasted_iota(jnp.int32, x.shape, axis) // bit) % bits
+        out = None
+        for p in range(bits):
+            moved = pltpu.roll(x, ((2 * p - bits + 1) * bit) % size, axis)
+            out = moved if out is None else jnp.where(index == p, moved, out)
+        return out
+
+    def mirror_lanes(x):
+        for bit, bits in ((1, 4), (4, 4), (16, 4), (64, 2)):
+            x = swap(x, bit, bits, 1)
+        return x
+
+    def mirror(x):
+        return swap(mirror_lanes(x), 1, 8, 0)
+
+    def end_rows():
+        loads[4].wait()
+        for side, _, r in edges:
+            for k in range(LEVELS):
+                vel_out[side, 0, pl.ds(k, 1), :] = tr[k, pl.ds(r, 1), :]
+                vel_out[side, 1, pl.ds(k, 1), :] = vr[k, pl.ds(r, 1), :]
+
+        @pl.when(is_top)
+        def _():
+            folded_out[...] = mirror_lanes(vel_out[1, 0])
+
+        @pl.when(not_top)
+        def _():
+            folded_out[...] = vel_out[1, 0]
+
+        vel_send[0] = vel_out[0]
+        vel_send[1, 0] = folded_out[...]
+        vel_send[1, 1] = vel_out[1, 1]
 
     pl.semaphore_wait(barrier, greeted)
 
-    def exchange(phase, beside_from, to_east, to_west, rows_from, rows_to, corners):
-        def by_rows(slot, side, wide, place, to_lon, to_lat):
-            src, dst = rows_from(side), rows_to.at[place]
-            if not wide:
-                src, dst = corners(src), corners(dst)
-            return remote(
-                "halo", src, dst, rows_send.at[phase, slot], rows_recv.at[phase, place],
-                {"lon": to_lon, "lat": to_lat})
-
-        go_e = remote(
-            "halo", beside_from, to_east, beside_send.at[phase, 0], beside_recv.at[phase, 0],
-            {"lon": east, "lat": lat})
-        go_w = remote(
-            "halo", beside_from, to_west, beside_send.at[phase, 1], beside_recv.at[phase, 1],
-            {"lon": west, "lat": lat})
-        go_up = by_rows(0, 1, True, jnp.where(is_top, 3, 0), up_lon, up_lat)
-        go_up_e = by_rows(1, 1, False, jnp.where(is_top, 5, 1), up_e, up_lat)
-        go_up_w = by_rows(2, 1, False, jnp.where(is_top, 4, 2), up_w, up_lat)
-        go_down = by_rows(3, 0, True, 3, lon, down_lat)
-        go_down_e = by_rows(4, 0, False, 4, east, down_lat)
-        go_down_w = by_rows(5, 0, False, 5, west, down_lat)
-        stay_e = local_copy(
-            "halo", corners(rows_from(1)), corners(rows_to.at[5]), rows_recv.at[phase, 5])
-        stay_w = local_copy(
-            "halo", corners(rows_from(1)), corners(rows_to.at[4]), rows_recv.at[phase, 4])
-        go_e.start()
-        go_w.start()
-        go_up.start()
-        pl.when(other_e)(go_up_e.start)
-        pl.when(other_w)(go_up_w.start)
-        pl.when(self_e)(stay_e.start)
-        pl.when(self_w)(stay_w.start)
-
-        @pl.when(not_bottom)
-        def _():
-            go_down.start()
-            go_down_e.start()
-            go_down_w.start()
-
-        def sent():
-            go_e.wait_send()
-            go_w.wait_send()
-            go_up.wait_send()
-            pl.when(other_e)(go_up_e.wait_send)
-            pl.when(other_w)(go_up_w.wait_send)
-
-            @pl.when(not_bottom)
-            def _():
-                go_down.wait_send()
-                go_down_e.wait_send()
-                go_down_w.wait_send()
-
-        def received():
-            arrived("halo", to_east, beside_recv.at[phase, 0])
-            arrived("halo", to_west, beside_recv.at[phase, 1])
-            arrived("halo", rows_to.at[3], rows_recv.at[phase, 3])
-            arrived("halo", corners(rows_to.at[4]), rows_recv.at[phase, 4])
-            arrived("halo", corners(rows_to.at[5]), rows_recv.at[phase, 5])
-
-            @pl.when(not_bottom)
-            def _():
-                arrived("halo", rows_to.at[0], rows_recv.at[phase, 0])
-                arrived("halo", corners(rows_to.at[1]), rows_recv.at[phase, 1])
-                arrived("halo", corners(rows_to.at[2]), rows_recv.at[phase, 2])
-
-        return sent, received
-
-    first_sent, first_received = exchange(
-        0, beside_out, beside_w, beside_e, lambda side: rows_out.at[side], rows_in,
-        lambda ref: ref.at[pl.ds(0, 2)])
+    depth_sent, depth_received = exchange(
+        0, beside_out, beside_w, beside_e, rows_out, rows_in, True)
+    ends_sent, ends_received = exchange(
+        1, ends_out, ends_w, ends_e, vel_send, vel_in, False, end_rows)
+
+    nothing = jnp.zeros(tile, jnp.float32)
+    for r in (south - 8, top + 8):
+        at = pl.ds(r, 8)
+        for half in range(2):
+            for buffer in (lv, w_n, w_ne, w_nw):
+                buffer[half, at, :] = nothing
+            for k in range(ITERS + 1):
+                basis[k, half, at, :] = nothing
 
     def tracer_rows(r, n, carry):
         at, up, down = pl.ds(r, n), pl.ds(r + 1, n), pl.ds(r - 1, n)
@@ -449,82 +483,66 @@
 
     sweep("tracer", GHOST, rows, TRACER_STEP, tracer_rows)
 
-    first_received()
+    depth_received()
 
     def clear(buffer):
-        for place in range(3):
+        for place in range(buffer.shape[0] // 2):
             buffer[place] = jnp.zeros(buffer.shape[1:], buffer.dtype)
 
     pl.when(jnp.logical_not(not_bottom))(lambda: clear(rows_in))
-
-    def swap(x, bit, axis):
-        size = x.shape[axis]
-        index = lax.broadcasted_iota(jnp.int32, x.shape, axis)
-        low = (index // bit) % 2 == 0
-        return jnp.where(low, pltpu.roll(x, size - bit, axis), pltpu.roll(x, bit, axis))
-
-    def mirror_lanes(x):
-        for bit in (1, 2, 4, 8, 16, 32, 64):
-            x = swap(x, bit, 1)
-        return x
-
-    def mirror(x):
-        x = mirror_lanes(x)
-        for bit in (1, 2, 4):
-            x = swap(x, bit, 0)
-        return x
 
     @pl.when(is_top)
     def _():
         for place in (3, 4, 5):
             for field in range(2):
                 rows_in[place, field] = mirror(rows_in[place, field])
-        rows_in[3, 2] = mirror_lanes(rows_in[3, 2])
+
+    shared_n = jnp.minimum(rows_out[1, 0][7:8], rows_in[3, 0][0:1])
+    shared_s = jnp.minimum(rows_out[0, 0][0:1], rows_in[0, 0][7:8])
+    lane_p = lanes(part)
+    even = lane_p % 2 == 0
+    d_mine, d_w, d_e = (buffer[at_l, :] for buffer in (beside_out, beside_w, beside_e))
+    both = jnp.where(
+        lane_p % 16 == 7, jnp.minimum(d_mine, roll(d_e, -1)),
+        jnp.where(lane_p % 16 == 8, jnp.minimum(roll(d_w, 1), d_mine), 0.0))
+    for half in range(2):
+        shared = jnp.where((lane_p // 16) % 2 == half, both, 0.0)
+        shared = roll(shared, -7 - 16 * half)
+        for shift in (2, 4, 8):
+            shared = shared + roll(shared, shift)
+        flux[pl.ds(half * part, part), :] = shared
+
+    ends_received()
+    pl.when(jnp.logical_not(not_bottom))(lambda: clear(vel_in))
 
     level_row = row.astype(jnp.float32)
     carry_north = jnp.where(is_top, 0.0, 1.0)
-    own_first, own_last = rows_out[0], rows_out[1]
-    shared_n = jnp.minimum(own_last[0][7:8], rows_in[3, 0][0:1])
+    own_first, own_last = vel_out[0], vel_out[1]
     flux_n = jnp.where(
         shared_n > level_row,
-        0.0625 * (1.92 * (rows_in[3, 2] - own_last[2])
-                  - carry_north * (own_last[3] + rows_in[3, 3]) * (own_last[2] + rows_in[3, 2])),
+        0.0625 * (1.92 * (vel_in[3, 0] - own_last[0])
+                  - carry_north * (own_last[1] + vel_in[3, 1]) * (own_last[0] + vel_in[3, 0])),
         0.0)
-    shared_s = jnp.minimum(own_first[0][0:1], rows_in[0, 0][7:8])
     flux_s = jnp.where(
         shared_s > level_row,
-        0.0625 * (1.92 * (own_first[2] - rows_in[0, 2])
-                  - (own_first[3] + rows_in[0, 3]) * (own_first[2] + rows_in[0, 2])),
+        0.0625 * (1.92 * (own_first[0] - vel_in[0, 0])
+                  - (own_first[1] + vel_in[0, 1]) * (own_first[0] + vel_in[0, 0])),
         0.0)
     first_own, last_own = pl.ds(0, 8), pl.ds(rows - 8, 8)
-    for k in range(LEVELS):
-        nt[k, last_own, :] = nt[k, last_own, :] + jnp.where(row == 7, flux_n[k:k + 1], 0.0)
-        nt[k, first_own, :] = nt[k, first_own, :] - jnp.where(row == 0, flux_s[k:k + 1], 0.0)
     total[last_own, :] = total[last_own, :] + jnp.where(
         row == 7, jnp.sum(flux_n, axis=0, keepdims=True), 0.0)
     total[first_own, :] = total[first_own, :] - jnp.where(
         row == 0, jnp.sum(flux_s, axis=0, keepdims=True), 0.0)
 
-    depths = [buffer[at_l, :] for buffer in (beside_out, beside_w, beside_e)]
     for half in range(2):
         at = pl.ds(half * part, part)
-        lane_p = lanes(part)
-        even = lane_p % 2 == 0
-        mine, from_w, from_e = beside_out[at, :], beside_w[at, :], beside_e[at, :]
+        mine, from_w, from_e = ends_out[at, :], ends_w[at, :], ends_e[at, :]
         here = jnp.where(even, mine, roll(from_w, 1))
         there = jnp.where(even, roll(from_e, -1), mine)
         carried = roll(here + there, -16) * (here + there)
-        d_mine, d_w, d_e = depths
-        shared = jnp.where(
-            lane_p % 16 == 7, jnp.minimum(d_mine, roll(d_e, -1)),
-            jnp.where(lane_p % 16 == 8, jnp.minimum(roll(d_w, 1), d_mine), 0.0))
-        shared = jnp.where((lane_p // 16) % 2 == half, shared, 0.0)
-        shared = roll(shared, -7 - 16 * half)
-        for shift in (2, 4, 8):
-            shared = shared + roll(shared, shift)
         level = ((lane_p % 16) // 2).astype(jnp.float32)
         through = jnp.where(
-            jnp.logical_and(shared > level, lane_p % 32 < 16),
+            jnp.logical_and(flux[at, :] > level, lane_p % 32 < 16),
             0.0625 * (1.92 * (there - here) - carried), 0.0)
         through = jnp.where(even, through, -through)
         flux[at, :] = through
@@ -542,12 +560,12 @@
         basis[0, 0, part_rows(c), :] = value
         return value
 
+    loads[5].wait()
     edge_out[...] = fold([right_side(c) for c in range(PARTS)])
     for side, r, _ in edges:
         edge_rows_out[side] = basis[0, 0, pl.ds(r, GHOST), :]
-    second_sent, second_received = exchange(
-        1, edge_out, edge_w, edge_e, lambda side: edge_rows_out.at[side], edge_rows,
-        lambda ref: ref)
+    side_sent, side_received = exchange(
+        2, edge_out, edge_w, edge_e, edge_rows_out, edge_rows, True)
 
     def place_rows(buffer, get):
         for r, across, w_at, e_at in ((south, 0, 1, 2), (top, 3, 4, 5)):
@@ -617,10 +635,13 @@
         return carry
 
     sweep("new", 0, 2 * part, part, ends_rows)
+    for k in range(LEVELS):
+        nt[k, last_own, :] = nt[k, last_own, :] + jnp.where(row == 7, flux_n[k:k + 1], 0.0)
+        nt[k, first_own, :] = nt[k, first_own, :] - jnp.where(row == 0, flux_s[k:k + 1], 0.0)
     out_new = local_copy("out", nt, new_out, out_sem.at[0])
     out_new.start()
 
-    second_received()
+    side_received()
     pl.when(jnp.logical_not(not_bottom))(lambda: clear(edge_rows))
 
     @pl.when(is_top)
@@ -755,8 +776,9 @@
     out_surf.start()
     out_res.start()
 
-    first_sent()
-    second_sent()
+    depth_sent()
+    ends_sent()
+    side_sent()
     for copy in sends:
         copy.wait_send()
     out_new.wait()
@@ -792,7 +814,7 @@
     cube = vmem(LEVELS, rows + 2 * GHOST, LANES)
     pair = vmem(2, *flat)
     block = vmem(rows, LANES)
-    beside = vmem(4 * part, LANES)
+    beside = vmem(2 * part, LANES)
     edge = vmem(part, LANES)
     dma = pltpu.SemaphoreType.DMA
     anywhere = pl.BlockSpec(memory_space=pl.ANY)
@@ -808,13 +830,15 @@
         out_specs=(anywhere,) * 3,
         scratch_shapes=[
             cube, cube, cube, vmem(rows, LANES, dtype=jnp.int32), block, pair, pair,
-            beside, beside, beside, vmem(2, 4, 8, LANES), vmem(6, 4, 8, LANES),
+            beside, beside, beside, vmem(2, 2, 8, LANES), vmem(6, 2, 8, LANES),
+            beside, beside, beside, vmem(2, 2, 8, LANES), vmem(2, 2, 8, LANES),
+            vmem(6, 2, 8, LANES), vmem(8, LANES),
             edge, edge, edge, vmem(2, 8, LANES), vmem(6, 8, LANES),
             vmem(2 * part, LANES), vmem(2 * part, LANES), block, vmem(LEVELS, rows, LANES),
             pair, pair, pair, pair, pair, pair, pair, pair, vmem(*flat),
             vmem(ITERS + 1, 2, *flat),
             block, block,
-            dma((6,)), dma((2, 6)), dma((2, 6)), dma((2, 2)), dma((2, 2)),
+            dma((6,)), dma((3, 6)), dma((3, 6)), dma((3, 2)), dma((3, 2)),
             dma((len(sizes), max(sizes))), dma((len(sizes), max(sizes))), dma((3,)),
             *[vmem(size, 1, LANES) for size in sizes],
         ],

time: 35.3 us -> 34.3 us (0.972)
  Pallas kernels: 34.5 us -> 33.5 us
    pallas_call x1, Pallas kernels: 32.2 us -> 31.1 us  [local(): pl.pallas_call(functools.partial(kernel, lon_count, lat_count, rows), out...]
where the time goes in v5:
time: 34.3 us; the launch traced here: 34.1 us
  Pallas kernels  33.5 us (98%)
  between operations  0.64 us (2%)
    pallas_call x1, Pallas kernels, local(): pl.pallas_call(functools.partial(kernel, lon_count, lat_count, rows), out...  31.1 us
    pallas_call x1, Pallas kernels, local(): pl.pallas_call(hand_over, out_shape=outs, in_specs=[anywhere] * 3, out_sp...  2.35 us

profile of v5, /device:TPU:0, one launch (start us, length us, event | category | flops | bytes accessed | tf_op | source)
XLA Modules:
  0.0 34.1 jit_solution(184442746902262502)
XLA Ops:
  0.6 31.1 %ocean_step.1 = (f32[8,320,128]{2,1,0:T(8,128)}, f32[320,128]{1,0:T(8,128)}, f32[320,128]{1,0:T(8,128)}) custom-call(f32[8,320,128]{2,1,0:T(8,128)} %t_in.1, f32[8,320,128]{2,1,0:T(8,128)} %u_in.1, f32[8,320,128]{2,1,0:T(8,128)} %v_in.1, s32[320,128]{1,0:T(8,128)} %lev_in.1, f32[320,128]{1,0:T(8,128)} %forc_in.1, f32[320,128]{1,0:T(8,128)} %stor_in.1), custom_call_target="tpu_custom_call" | custom-call | flops 100000000 | bytes 6000000 | tf_op jit(solution)/shard_map/ocean_step/pallas_call | solution.py:826
  31.8 2.3 %hand_over.1 = (f32[8,320,128]{2,1,0:T(8,128)}, f32[320,128]{1,0:T(8,128)}, f32[320,128]{1,0:T(8,128)}) custom-call(f32[8,320,128]{2,1,0:T(8,128)} %get-tuple-element.6.new, f32[320,128]{1,0:T(8,128)} %get-tuple-element.7.surf, f32[320,128]{1,0:T(8,128)} %get-tuple-element.8.res), custom_call_target="tpu_custom_call" | custom-call | tf_op jit(solution)/shard_map/hand_over/pallas_call | solution.py:851

commit v6 on v5

--- a/solution.py
+++ b/solution.py
@@ -18,12 +18,12 @@
 SCALE = 0.8
 MESH = pl.DeviceIdType.MESH
 STAGES = (("core", "y"), ("x", "z"))
-TRACER_STEP = 16
-WEIGHTS_STEP = 112
+TRACER_STEP = 32
+WEIGHTS_STEP = 168
 DIAGONAL_STEP = 48
-SCALED_STEP = 112
-APPLY_STEP = 112
-LAST_STEP = 160
+SCALED_STEP = 336
+APPLY_STEP = 168
+LAST_STEP = 320
 FINAL_STEP = 80
 
 GAIN = (-1.0, 1.0 / SCALE, 2.0 / SCALE, 2.0 / SCALE, 2.0 / SCALE)
@@ -394,7 +394,7 @@
         ends_out[pl.ds(r, n), :] = out
         return carry
 
-    sweep("ends", 0, 2 * part, part, pack_ends)
+    sweep("ends", 0, 2 * part, 2 * part, pack_ends)
     def swap(x, bit, bits, axis):
         size = x.shape[axis]
         index = (lax.broadcasted_iota(jnp.int32, x.shape, axis) // bit) % bits

time: 34.3 us -> 33.8 us (0.985)
  Pallas kernels: 33.5 us -> 33 us
    pallas_call x1, Pallas kernels: 31.1 us -> 30.7 us  [local(): pl.pallas_call(functools.partial(kernel, lon_count, lat_count, rows), out...]
where the time goes in v6:
time: 33.8 us; the launch traced here: 33.6 us
  Pallas kernels  33 us (98%)
  between operations  0.64 us (2%)
    pallas_call x1, Pallas kernels, local(): pl.pallas_call(functools.partial(kernel, lon_count, lat_count, rows), out...  30.7 us
    pallas_call x1, Pallas kernels, local(): pl.pallas_call(hand_over, out_shape=outs, in_specs=[anywhere] * 3, out_sp...  2.35 us

profile of v6, /device:TPU:0, one launch (start us, length us, event | category | flops | bytes accessed | tf_op | source)
XLA Modules:
  0.0 33.6 jit_solution(9762831011680538010)
XLA Ops:
  0.6 30.7 %ocean_step.1 = (f32[8,320,128]{2,1,0:T(8,128)}, f32[320,128]{1,0:T(8,128)}, f32[320,128]{1,0:T(8,128)}) custom-call(f32[8,320,128]{2,1,0:T(8,128)} %t_in.1, f32[8,320,128]{2,1,0:T(8,128)} %u_in.1, f32[8,320,128]{2,1,0:T(8,128)} %v_in.1, s32[320,128]{1,0:T(8,128)} %lev_in.1, f32[320,128]{1,0:T(8,128)} %forc_in.1, f32[320,128]{1,0:T(8,128)} %stor_in.1), custom_call_target="tpu_custom_call" | custom-call | flops 100000000 | bytes 6000000 | tf_op jit(solution)/shard_map/ocean_step/pallas_call | solution.py:826
  31.3 2.3 %hand_over.1 = (f32[8,320,128]{2,1,0:T(8,128)}, f32[320,128]{1,0:T(8,128)}, f32[320,128]{1,0:T(8,128)}) custom-call(f32[8,320,128]{2,1,0:T(8,128)} %get-tuple-element.6.new, f32[320,128]{1,0:T(8,128)} %get-tuple-element.7.surf, f32[320,128]{1,0:T(8,128)} %get-tuple-element.8.res), custom_call_target="tpu_custom_call" | custom-call | tf_op jit(solution)/shard_map/hand_over/pallas_call | solution.py:851

commit v7 on v6

--- a/solution.py
+++ b/solution.py
@@ -20,11 +20,11 @@
 STAGES = (("core", "y"), ("x", "z"))
 TRACER_STEP = 32
 WEIGHTS_STEP = 168
-DIAGONAL_STEP = 48
+DIAGONAL_STEP = 168
 SCALED_STEP = 336
-APPLY_STEP = 168
+APPLY_STEP = 336
 LAST_STEP = 320
-FINAL_STEP = 80
+FINAL_STEP = 320
 
 GAIN = (-1.0, 1.0 / SCALE, 2.0 / SCALE, 2.0 / SCALE, 2.0 / SCALE)
 SHIFT = (1.0, 0.0, 0.0, 0.0, 0.0)

time: 33.8 us -> 33.7 us (level)
  no operation moved by 1% of the time
where the time goes in v7:
time: 33.7 us; the launch traced here: 33.5 us
  Pallas kernels  32.9 us (98%)
  between operations  0.64 us (2%)
    pallas_call x1, Pallas kernels, local(): pl.pallas_call(functools.partial(kernel, lon_count, lat_count, rows), out...  30.6 us
    pallas_call x1, Pallas kernels, local(): pl.pallas_call(hand_over, out_shape=outs, in_specs=[anywhere] * 3, out_sp...  2.35 us

profile of v7, /device:TPU:0, one launch (start us, length us, event | category | flops | bytes accessed | tf_op | source)
XLA Modules:
  0.0 33.5 jit_solution(16497779453113619178)
XLA Ops:
  0.6 30.6 %ocean_step.1 = (f32[8,320,128]{2,1,0:T(8,128)}, f32[320,128]{1,0:T(8,128)}, f32[320,128]{1,0:T(8,128)}) custom-call(f32[8,320,128]{2,1,0:T(8,128)} %t_in.1, f32[8,320,128]{2,1,0:T(8,128)} %u_in.1, f32[8,320,128]{2,1,0:T(8,128)} %v_in.1, s32[320,128]{1,0:T(8,128)} %lev_in.1, f32[320,128]{1,0:T(8,128)} %forc_in.1, f32[320,128]{1,0:T(8,128)} %stor_in.1), custom_call_target="tpu_custom_call" | custom-call | flops 100000000 | bytes 6000000 | tf_op jit(solution)/shard_map/ocean_step/pallas_call | solution.py:826
  31.2 2.3 %hand_over.1 = (f32[8,320,128]{2,1,0:T(8,128)}, f32[320,128]{1,0:T(8,128)}, f32[320,128]{1,0:T(8,128)}) custom-call(f32[8,320,128]{2,1,0:T(8,128)} %get-tuple-element.6.new, f32[320,128]{1,0:T(8,128)} %get-tuple-element.7.surf, f32[320,128]{1,0:T(8,128)} %get-tuple-element.8.res), custom_call_target="tpu_custom_call" | custom-call | tf_op jit(solution)/shard_map/hand_over/pallas_call | solution.py:851
